TPU v7x, 128 devices: a whole 4x4x4 slice. The times are simulated.
128 devices in a mesh: view: 8 (over y, x_hi), tile: 16 (over z, x_lo, core).
Axes of the slice: x: 4 (x_hi: 2, x_lo: 2; x = x_hi * 2 + x_lo), y: 4, z: 4, core: 2. Of those that a mesh axis runs over, the one named last changes fastest.
Arguments:
- object_band: float32 [16, 2, 1024, 128], P('view', None, 'tile'), may hold values from -6 to 6
- dual_band: float32 [16, 2, 1024, 128], P('view', None, 'tile'), may hold values from -6 to 6
- probe_field: float32 [2, 128, 128], replicated, may hold values from -6 to 6
- positions: int32 [16, 512], P('view', 'tile'), may hold values from 0 to 63
- live_counts: int32 [16, 16], P('view', 'tile'), may hold values from 1 to 32, 170 in all within a row
- photon_counts: int32 [16, 512, 128, 128], P('view', 'tile'), may hold values from 0 to 1023
- footprints: int32 [16, 16], P('view', 'tile'), may hold values from 0 to 14
- weights: bfloat16 [16, 128, 131072], P('view', None, 'tile'), may hold values from -0.046875 to 0.046875
- volume: float32 [2, 1024, 128, 128], P(None, 'tile'), may hold values from -6 to 6
Outputs:
- object_new: float32 [16, 2, 1024, 128], P('view', None, 'tile')
- dual_new: float32 [16, 2, 1024, 128], P('view', None, 'tile')
- volume_new: float32 [2, 1024, 128, 128], P(None, 'tile')
Inputs may be any that keep to these rules, and one draw needn't show every extreme that they name: `positions`: offset of a slot's scan position from the first column of the tile that owns the slot. `live_counts`: the first that many of a tile's 32 slots are live; each view has exactly 170 live slots, and in each view some tile has all 32 live. `footprints`: first of the 2 consecutive detector tiles that a volume tile's shadow covers in a view.
All inputs are finite; a program needn't handle non-finite values. No bound on the sum of `live_counts` on one device may be relied on, other than what follows from the above.
Results may differ from a plain program's by a relative error of at most 0.006.
Values may be sent and summed in bfloat16 or wider, within the bound.
A program may use at most 128 MiB of HBM per device.

v0:
```python
import jax
import jax.numpy as jnp
from jax import lax
from jax.sharding import PartitionSpec as P

rho_weight = 0.5
step_size = 0.5
prior_weight = 0.5
floor_term = 0.25


def passed_along(value, axis, steps):
    count = lax.axis_size(axis)
    initial, last = (max(0, -steps), min(count, count - steps))
    return lax.ppermute(value, axis, [(source, source + steps) for source in range(initial, last)])


def from_everyone(array, axis):
    devices = lax.axis_size(axis)
    return lax.all_to_all(
        jnp.broadcast_to(array[None], (devices, *array.shape)), axis, 0, 0, tiled=True
    )


def laid_out(blocks, dim):
    blocks = jnp.moveaxis(blocks, 0, dim)
    shape = blocks.shape
    return blocks.reshape(*shape[:dim], shape[dim] * shape[dim + 1], *shape[dim + 2 :])


def gathered_copies(array, axis, dim):
    blocks = from_everyone(array, axis)
    return laid_out(blocks, dim)


def with_halo(array, sides, width):
    edges = {}
    for axis, dim in sides:
        devices, length = (lax.axis_size(axis), array.shape[dim])
        up = [(i, (i + 1) % devices) for i in range(devices - 1)]
        last = lax.slice_in_dim(array, length - width, length, axis=dim)
        initial = lax.slice_in_dim(array, 0, width, axis=dim)
        edges[dim] = (
            lax.ppermute(last, axis, up),
            lax.ppermute(initial, axis, [(b, a) for a, b in up]),
        )
    done = []
    for _, dim in sides:
        low, high = edges[dim]
        around = [(width, width) if d in done else (0, 0) for d in range(array.ndim)]
        array = jnp.concatenate([jnp.pad(low, around), array, jnp.pad(high, around)], axis=dim)
        done.append(dim)
    return array


def tables(order_n):
    counter = jnp.arange(order_n, dtype=jnp.int32)
    phase_index = counter[:, None] * counter[None, :] % order_n
    angles = phase_index.astype(jnp.float32) * (2.0 * jnp.pi / order_n)
    scaling = 1.0 / jnp.sqrt(jnp.float32(order_n))
    return (jnp.cos(angles) * scaling, -jnp.sin(angles) * scaling)


def block_minus(parts):
    upper_half = jnp.concatenate([parts[0], -parts[1]], axis=1)
    lower_half = jnp.concatenate([parts[1], parts[0]], axis=1)
    return jnp.concatenate([upper_half, lower_half], axis=0).astype(jnp.bfloat16)


def block_plus(parts):
    upper_half = jnp.concatenate([parts[0], parts[1]], axis=1)
    lower_half = jnp.concatenate([-parts[1], parts[0]], axis=1)
    return jnp.concatenate([upper_half, lower_half], axis=0).astype(jnp.bfloat16)


def markov(padded):
    centre = padded[:, 1:-1, 1:-1, 1:-1]
    summed = jnp.zeros_like(centre)
    neighbours = (
        padded[:, 2:, 1:-1, 1:-1],
        padded[:, :-2, 1:-1, 1:-1],
        padded[:, 1:-1, 2:, 1:-1],
        padded[:, 1:-1, :-2, 1:-1],
        padded[:, 1:-1, 1:-1, 2:],
        padded[:, 1:-1, 1:-1, :-2],
    )
    for neighbour in neighbours:
        difference = centre - neighbour
        summed = summed + difference / jnp.sqrt(1.0 + difference * difference)
    return summed


def batch_update(windows, probe_field, counts_grid, dft_blocks):
    left_a, right_b, right_a, left_b = dft_blocks
    probe_re = probe_field[0]
    probe_im = probe_field[1]
    obj_re = windows[:, 0]
    obj_im = windows[:, 1]
    exit_wave = jnp.stack(
        [probe_re * obj_re - probe_im * obj_im, probe_re * obj_im + probe_im * obj_re], axis=1
    ).astype(jnp.bfloat16)
    num_slots = exit_wave.shape[0]
    num_cols = exit_wave.shape[2]
    num_rows = exit_wave.shape[3]
    columns_done = jnp.einsum(
        "ab,sbh->sah",
        left_a,
        exit_wave.reshape(num_slots, 2 * num_cols, num_rows),
        preferred_element_type=jnp.float32,
    ).astype(jnp.bfloat16)
    columns_done = (
        columns_done.reshape(num_slots, 2, num_cols, num_rows)
        .transpose(0, 2, 1, 3)
        .reshape(num_slots, num_cols, 2 * num_rows)
    )
    spectrum = jnp.einsum("sph,hq->spq", columns_done, right_b, preferred_element_type=jnp.float32)
    amplitude = jnp.sqrt(counts_grid.astype(jnp.float32)) / 16.0
    spec_re = spectrum[:, :, :num_rows]
    spec_im = spectrum[:, :, num_rows:]
    factor = amplitude / jnp.sqrt(spec_re * spec_re + spec_im * spec_im + floor_term)
    replaced = (spectrum * jnp.concatenate([factor, factor], axis=2)).astype(jnp.bfloat16)
    inverse_rows = jnp.einsum(
        "spq,qh->sph", replaced, right_a, preferred_element_type=jnp.float32
    ).astype(jnp.bfloat16)
    inverse_rows = (
        inverse_rows.reshape(num_slots, num_cols, 2, num_rows)
        .transpose(0, 2, 1, 3)
        .reshape(num_slots, 2 * num_cols, num_rows)
    )
    new_wave = jnp.einsum(
        "ab,sbh->sah", left_b, inverse_rows, preferred_element_type=jnp.float32
    ).reshape(num_slots, 2, num_cols, num_rows)
    difference = new_wave - exit_wave.astype(jnp.float32)
    diff_re = difference[:, 0]
    diff_im = difference[:, 1]
    power = jnp.broadcast_to(probe_re * probe_re + probe_im * probe_im, diff_re.shape)
    return jnp.stack(
        [probe_re * diff_re + probe_im * diff_im, probe_re * diff_im - probe_im * diff_re, power],
        axis=2,
    )


def place_windows(shadows, footprints, tile_cols, band_cols):
    placed = []
    for view_index in range(shadows.shape[0]):
        blank = jnp.zeros((shadows.shape[1], band_cols, shadows.shape[3]), jnp.float32)
        first_col = footprints[view_index, 0] * tile_cols
        placed.append(lax.dynamic_update_slice_in_dim(blank, shadows[view_index], first_col, 1))
    return jnp.stack(placed)


def cut_windows(full_band, footprints, tile_cols, foot_cols):
    pieces = []
    for view_index in range(full_band.shape[0]):
        first_col = footprints[view_index, 0] * tile_cols
        pieces.append(lax.dynamic_slice_in_dim(full_band[view_index], first_col, foot_cols, 1))
    return jnp.stack(pieces)


def per_device(
    object_band,
    dual_band,
    probe_field,
    positions,
    live_counts,
    photon_counts,
    footprints,
    weights,
    volume,
):
    views_here = object_band.shape[0]
    tile_cols = object_band.shape[2]
    band_rows = object_band.shape[3]
    patch_cols = probe_field.shape[1]
    slots_here = positions.shape[1]
    band_cols = tile_cols * lax.axis_size("tile")
    foot_cols = weights.shape[1]
    voxels_here = weights.shape[2]
    depth_rows = volume.shape[2]
    dft_blocks = (
        block_minus(tables(patch_cols)),
        block_plus(tables(band_rows)),
        block_minus(tables(band_rows)),
        block_plus(tables(patch_cols)),
    )
    volume_low = volume.astype(jnp.bfloat16).reshape(2, voxels_here, band_rows)
    shadows = jnp.einsum("acx,kxh->akch", weights, volume_low, preferred_element_type=jnp.float32)
    placed = place_windows(shadows, footprints, tile_cols, band_cols)
    projection = lax.psum_scatter(placed, "tile", scatter_dimension=2, tiled=True)
    ahead_one = passed_along(object_band, "tile", -1)
    ahead_two = passed_along(object_band, "tile", -2)
    reach = jnp.concatenate([object_band, ahead_one, ahead_two], axis=2)
    slot_rank = jnp.arange(slots_here, dtype=jnp.int32)
    patch_rank = jnp.arange(patch_cols, dtype=jnp.int32)
    reach_rank = jnp.arange(3 * tile_cols, dtype=jnp.int32)
    updates = []
    for view_index in range(views_here):
        view_reach = reach[view_index]
        offsets = positions[view_index]
        windows = jax.vmap(
            lambda offset_col: lax.dynamic_slice_in_dim(view_reach, offset_col, patch_cols, 1)
        )(offsets)
        contrib = batch_update(windows, probe_field, photon_counts[view_index], dft_blocks)
        is_live = (slot_rank < live_counts[view_index, 0]).astype(jnp.float32)
        target_col = offsets[:, None] + patch_rank[None, :]
        placement = (target_col[:, :, None] == reach_rank[None, None, :]).astype(
            jnp.float32
        ) * is_live[:, None, None]
        placement = placement.reshape(slots_here * patch_cols, 3 * tile_cols)
        flat = contrib.reshape(slots_here * patch_cols, 3 * band_rows)
        gathered_cols = jnp.dot(
            placement.T, flat, precision=lax.Precision.HIGHEST, preferred_element_type=jnp.float32
        )
        updates.append(gathered_cols.reshape(3 * tile_cols, 3, band_rows).transpose(1, 0, 2))
    local_updates = jnp.stack(updates)
    own_part = local_updates[:, :, :tile_cols]
    from_one = passed_along(
        local_updates[:, :, tile_cols : 2 * tile_cols].astype(jnp.bfloat16), "tile", 1
    ).astype(jnp.float32)
    from_two = passed_along(
        local_updates[:, :, 2 * tile_cols :].astype(jnp.bfloat16), "tile", 2
    ).astype(jnp.float32)
    summed_update = own_part + from_one + from_two
    object_new = (
        object_band
        + summed_update[:, 0:2] / (1.0 + summed_update[:, 2:3])
        - rho_weight * (object_band - projection - dual_band)
    )
    dual_new = dual_band + projection - object_new
    residual = (projection - object_new + dual_band).astype(jnp.bfloat16)
    residual_full = gathered_copies(residual, "tile", 2)
    residual_windows = cut_windows(residual_full, footprints, tile_cols, foot_cols)
    grad_part = jnp.einsum(
        "acx,akch->kxh", weights, residual_windows, preferred_element_type=jnp.float32
    ).reshape(2, tile_cols, depth_rows, band_rows)
    share_rows = depth_rows // lax.axis_size("view")
    gradient = lax.psum_scatter(grad_part, "view", scatter_dimension=2, tiled=True)
    own_rows = lax.dynamic_slice_in_dim(volume, lax.axis_index("view") * share_rows, share_rows, 2)
    half_step = own_rows - step_size * gradient
    padded = with_halo(half_step, (("view", 2), ("tile", 1)), 1)
    padded = jnp.pad(padded, ((0, 0), (0, 0), (0, 0), (1, 1)))
    share_new = half_step - step_size * prior_weight * markov(padded)
    volume_new = lax.all_gather(share_new, "view", axis=2, tiled=True)
    return (object_new, dual_new, volume_new)


def solution(mesh):
    return jax.shard_map(
        per_device,
        mesh=mesh,
        in_specs=(
            P("view", None, "tile", None),
            P("view", None, "tile", None),
            P(),
            P("view", "tile"),
            P("view", "tile"),
            P("view", "tile", None, None),
            P("view", "tile"),
            P("view", None, "tile"),
            P(None, "tile", None, None),
        ),
        out_specs=(
            P("view", None, "tile", None),
            P("view", None, "tile", None),
            P(None, "tile", None, None),
        ),
        check_vma=False,
    )
```

profile of v0, /device:TPU:1, one launch (start us, length us, event | category | flops | bytes accessed | tf_op | source)
XLA Modules:
  0.0 534.6 jit_solution(18169835047681503835)
XLA Ops:
  8.3 3.3 collective-permute-start
  15.5 6.4 %convert_element_type.132 = bf16[2,64,128,128]{3,2,1,0:T(8,128)(2,1)} convert(f32[2,64,128,128]{3,2,1,0:T(8,128)} %param.17) | non-fusion elementwise | flops 2097152 | bytes 12582912 | tf_op jit(solution)/shard_map/convert_element_type | solution.py:186
  21.9 4.7 fusion.43
  33.9 6.9 %gather_fusion = f32[32,2,128,128]{3,1,2,0:T(2,128)} fusion(f32[2,192,128]{2,0,1:T(2,128)S(1)} %get-tuple-element.26, s32[32]{0:T(128)S(1)} %get-tuple-element.39), kind=kCustom, calls=%fused_computation | custom fusion | bytes 8388992 | tf_op jit(solution)/shard_map/vmap()/gather | solution.py:201
  40.8 9.2 %fusion.94 = (f32[32,1,128,128]{3,1,2,0:T(1,128)S(1)}, f32[32,1,128,128]{3,1,2,0:T(1,128)}) fusion(f32[32,2,128,128]{3,1,2,0:T(2,128)} %gather_fusion), kind=kLoop, calls=%fused_computation.167 | loop fusion | bytes 8388608 | tf_op jit(solution)/shard_map/slice | solution.py:98
  50.0 7.3 %gather_fusion.1 = f32[32,2,128,128]{3,1,2,0:T(2,128)} fusion(f32[2,192,128]{2,0,1:T(2,128)S(1)} %get-tuple-element.25, s32[32]{0:T(128)S(1)} %get-tuple-element.38), kind=kCustom, calls=%fused_computation.1 | custom fusion | bytes 8388992 | tf_op jit(solution)/shard_map/vmap()/gather | solution.py:201
  57.3 8.0 %fusion.93 = (f32[32,1,128,128]{3,1,2,0:T(1,128)S(1)}, f32[32,1,128,128]{3,1,2,0:T(1,128)S(1)}) fusion(f32[32,2,128,128]{3,1,2,0:T(2,128)} %gather_fusion.1), kind=kLoop, calls=%fused_computation.166 | loop fusion | bytes 8388608 | tf_op jit(solution)/shard_map/slice | solution.py:98
  65.3 2.1 multiply_subtract_fusion.1
  68.6 2.1 convert_bitcast_fusion
  70.7 4.0 reshape.294
  74.7 8.0 %copy.133 = bf16[32,128,2,128]{3,2,1,0:T(2,128)(2,1)} copy(bf16[32,128,2,128]{1,2,3,0:T(2,128)(2,1)} %bitcast.206) | data formatting | bytes 4194304 | tf_op jit(solution)/shard_map/transpose | solution.py:113
  82.7 4.4 reshape.295
  87.1 4.5 fusion.83
  95.9 8.0 %copy.124 = bf16[32,128,2,128]{3,2,1,0:T(2,128)(2,1)} copy(bf16[32,128,2,128]{1,2,3,0:T(2,128)(2,1)} %bitcast.207) | data formatting | bytes 4194304 | tf_op jit(solution)/shard_map/transpose | solution.py:113
  103.9 3.2 reshape.289
  109.2 4.8 fusion.19
  116.1 2.5 reshape.290
  118.6 6.6 %copy.125 = bf16[32,2,128,128]{2,1,3,0:T(2,128)(2,1)} copy(bf16[32,2,128,128]{3,1,2,0:T(2,128)(2,1)S(1)} %bitcast.208) | data formatting | bytes 4194304 | tf_op jit(solution)/shard_map/transpose | solution.py:127
  125.3 3.2 reshape.291
  128.4 2.7 convolution_bitcast_fusion.2
  131.2 5.7 %copy.126 = f32[32,256,128]{2,1,0:T(8,128)} copy(f32[32,256,128]{1,2,0:T(8,128)} %convolution_bitcast_fusion.2) | data formatting | bytes 8388608 | tf_op jit(solution)/shard_map/ab,sbh->sah/transpose | solution.py:130
  136.9 4.3 fusion.28
  141.2 2.5 reshape.296
  143.7 6.6 %copy.134 = bf16[32,2,128,128]{2,1,3,0:T(2,128)(2,1)} copy(bf16[32,2,128,128]{3,1,2,0:T(2,128)(2,1)S(1)} %bitcast.209) | data formatting | bytes 4194304 | tf_op jit(solution)/shard_map/transpose | solution.py:127
  150.3 3.2 reshape.297
  153.5 2.8 convolution_bitcast_fusion.1
  156.2 5.8 %copy.135 = f32[32,256,128]{2,1,0:T(8,128)} copy(f32[32,256,128]{1,2,0:T(8,128)} %convolution_bitcast_fusion.1) | data formatting | bytes 8388608 | tf_op jit(solution)/shard_map/ab,sbh->sah/transpose | solution.py:130
  162.0 3.0 convert_subtract_fusion
  168.8 5.4 %pad_maximum_fusion = (f32[32,128,3,128]{3,1,0,2:T(8,128)}, f32[32,128,3,128]{3,1,0,2:T(8,128)}) fusion(f32[32,128,1,128]{3,1,0,2:T(8,128)S(1)} %stack_broadcast_in_dim.4, f32[32,128,1,128]{3,1,0,2:T(8,128)S(1)} %get-tuple-element.6, f32[32,128,1,128]{3,1,0,2:T(8,128)S(1)} %get-tuple-element.5, f32[32,128,1,128]{3,1,0,2:T(8,128)S(1)} %get-tuple-element.29, ...), kind=kLoop, calls=%fused_computation.3 | loop fusion | flops 6291456 | bytes 23068672 | tf_op jit(solution)/shard_map/stack | solution.py:137
  174.2 6.7 %copy.137 = f32[32,128,3,128]{1,0,3,2:T(8,128)} copy(f32[32,128,3,128]{3,1,0,2:T(8,128)} %get-tuple-element.17) | data formatting | bytes 12582912 | tf_op jit(solution)/shard_map/stack | solution.py:137
  180.9 11.4 %copy.165 = f32[48,8,32,128]{3,1,2,0:T(8,128)} copy(f32[48,8,32,128]{3,2,1,0:T(8,128)} %bitcast.197) | data formatting | bytes 12582912
  192.3 6.9 %copy.128 = f32[32,128,3,128]{1,0,3,2:T(8,128)} copy(f32[32,128,3,128]{3,1,0,2:T(8,128)} %get-tuple-element.18) | data formatting | bytes 12582912 | tf_op jit(solution)/shard_map/stack | solution.py:137
  199.3 8.9 %copy.166 = f32[48,8,32,128]{3,1,2,0:T(8,128)S(1)} copy(f32[48,8,32,128]{3,2,1,0:T(8,128)} %bitcast.198) | data formatting | bytes 12582912
  208.3 6.6 %fusion.40 = f32[1,3,192,128]{3,2,1,0:T(8,128)S(1)} fusion(f32[3,128,4096]{2,1,0:T(8,128)S(1)} %bitcast.195, f32[4096]{0:T(1024)S(1)} %broadcast_bitcast_fusion, s32[4096]{0:T(1024)S(1)} %copy-done.19), kind=kOutput, calls=%fused_computation.74 | convolution fusion | flops 3625451520 | bytes 6619136 | tf_op jit(solution)/shard_map/dot_general | solution.py:211
  214.9 6.5 %fusion.37 = f32[1,3,192,128]{3,2,1,0:T(8,128)S(1)} fusion(f32[3,128,4096]{2,1,0:T(8,128)S(1)} %bitcast.196, f32[4096]{0:T(1024)S(1)} %broadcast_bitcast_fusion.1, s32[4096]{0:T(1024)S(1)} %get-tuple-element.47), kind=kOutput, calls=%fused_computation.73 | convolution fusion | flops 3625451520 | bytes 6619136 | tf_op jit(solution)/shard_map/dot_general | solution.py:211
  221.5 3.9 collective-permute-start.2
  225.4 4.5 collective-permute-start.3
  232.9 23.1 %all_to_all.5 = bf16[16,2,2,64,128]{4,3,2,1,0:T(8,128)(2,1)S(1)} all-to-all(bf16[16,2,2,64,128]{4,3,2,1,0:T(8,128)(2,1)S(1)} %broadcast_in_dim.2), channel_id=1, replica_groups=mesh['view'=8,'tile'=16] {'tile'}, dimensions={0} | all-to-all | bytes 2097152 | tf_op jit(solution)/shard_map/all_to_all | solution.py:20
  256.4 6.9 %convolution_bitcast_fusion = f32[2,8192,128]{1,2,0:T(8,128)} fusion(bf16[2,128,8192]{2,1,0:T(8,128)(2,1)} %param.16, bf16[1,2,128,128]{2,3,0,1:T(8,128)(2,1)S(1)} %bitcast.218, bf16[1,2,128,128]{2,3,0,1:T(8,128)(2,1)S(1)} %bitcast.217), kind=kOutput, calls=%fused_computation.2 | convolution fusion | flops 1073807360 | bytes 12713984 | tf_op jit(solution)/shard_map/acx,akch->kxh/dot_general | solution.py:233
  263.3 8.9 %copy.151 = f32[2,8192,128]{2,1,0:T(8,128)} copy(f32[2,8192,128]{1,2,0:T(8,128)} %convolution_bitcast_fusion) | data formatting | bytes 16777216 | tf_op jit(solution)/shard_map/reshape | solution.py:235
  272.3 113.5 %reduce-scatter.5.cloned.1.call-done = f32[2,64,16,128]{3,2,1,0:T(8,128)} async-done(((f32[2,64,128,128]{3,2,1,0:T(8,128)}), f32[2,64,16,128]{3,2,1,0:T(8,128)}) %reduce-scatter.5.cloned.1.call-update) | async-done | bytes 1048592 | tf_op jit(solution)/shard_map/reduce_scatter | solution.py:237
  387.6 2.1 collective-permute-start.4
  391.0 3.5 collective-permute-start.6
  394.5 3.0 collective-permute-start.7
  398.4 2.5 select_maximum_fusion
  400.9 2.8 multiply_subtract_fusion.3
  404.4 115.5 %all-gather.2.cloned.1.call-done = f32[2,64,128,128]{3,2,1,0:T(8,128)} async-done(((f32[2,64,16,128]{3,2,1,0:T(8,128)}), f32[2,64,128,128]{3,2,1,0:T(8,128)}) %all-gather.2.cloned.1.call-update) | async-done | bytes 8388624 | tf_op jit(solution)/shard_map/all_gather | solution.py:243
  519.9 7.9 %copy.175 = f32[2,64,128,128]{3,2,1,0:T(8,128)} copy(f32[2,64,128,128]{3,2,1,0:T(8,128)} %all-gather.2.cloned.1.call-done) | data formatting | bytes 16777216
  (117 shorter events, 32.3 us)
Async XLA Ops:
  7.2 224.5 %reduce-scatter.3.cloned.1.call-start = ((), (), s32[]{:S(2)}) async-start(), calls=%async_computation.3 | async-start | bytes 2228224 | tf_op jit(solution)/shard_map/reduce_scatter | solution.py:189
  8.3 25.5 %collective-permute-start = (f32[2,2,64,128]{3,1,2,0:T(2,128)S(1)}, f32[2,2,64,128]{3,1,2,0:T(2,128)S(1)}, u32[]{:S(2)}, u32[]{:S(2)}) collective-permute-start(f32[2,2,64,128]{3,1,2,0:T(2,128)S(1)} %get-tuple-element.34), channel_id=1, source_target_pairs={{1,0},{2,1},{3,2},{4,3},{5,4},{6,5},{7,6},{8,7},{9,8},{10,9},{11,1... | collective-permute-start | bytes 393224 | tf_op jit(solution)/shard_map/ppermute | solution.py:15
  11.6 22.2 %collective-permute-start.1 = (f32[2,2,64,128]{3,1,2,0:T(2,128)S(1)}, f32[2,2,64,128]{3,1,2,0:T(2,128)S(1)}, u32[]{:S(2)}, u32[]{:S(2)}) collective-permute-start(f32[2,2,64,128]{3,1,2,0:T(2,128)S(1)} %get-tuple-element.34), channel_id=1, source_target_pairs={{2,0},{3,1},{4,2},{5,3},{6,4},{7,5},{8,6},{9,7},{10,8},{11,9},{12,... | collective-permute-start | bytes 393224 | tf_op jit(solution)/shard_map/ppermute | solution.py:15
  28.3 0.9 copy-start.13
  28.3 2.2 copy-start.20
  28.3 2.2 copy-start.21
  28.4 357.4 %reduce-scatter.5.cloned.1.call-start = ((), (), s32[]{:S(2)}) async-start(), calls=%async_computation.4 | async-start | bytes 9437184 | tf_op jit(solution)/shard_map/reduce_scatter | solution.py:237
  57.3 8.0 %copy-start.1 = (f32[32,1,128,128]{3,1,2,0:T(1,128)S(1)}, f32[32,1,128,128]{3,1,2,0:T(1,128)}, u32[]{:S(2)}) copy-start(f32[32,1,128,128]{3,1,2,0:T(1,128)} %get-tuple-element.16) | copy-start | bytes 6291460
  57.3 8.0 %copy-start.11 = (f32[128,128]{1,0:T(8,128)S(1)}, f32[128,128]{1,0:T(8,128)}, u32[]{:S(2)}) copy-start(f32[128,128]{1,0:T(8,128)} %get-tuple-element.33) | copy-start | bytes 196612
  67.4 1.0 copy-start.4
  87.1 4.5 copy-start.2
  91.6 1.2 copy-start.6
  92.0 1.0 copy-start.8
  107.0 2.2 copy-start
  131.2 5.7 %copy-start.10 = (f32[32,128,128]{2,1,0:T(8,128)S(1)}, f32[32,128,128]{2,1,0:T(8,128)}, u32[]{:S(2)}) copy-start(f32[32,128,128]{2,1,0:T(8,128)} %get-tuple-element.11) | copy-start | bytes 6291460
  156.2 5.8 %copy-start.7 = (bf16[32,1,128,128]{3,2,1,0:T(8,128)(2,1)S(1)}, bf16[32,1,128,128]{3,2,1,0:T(8,128)(2,1)}, u32[]{:S(2)}) copy-start(bf16[32,1,128,128]{3,2,1,0:T(8,128)(2,1)} %get-tuple-element.31) | copy-start | bytes 3145732
  156.2 5.8 %copy-start.9 = (bf16[32,1,128,128]{3,2,1,0:T(8,128)(2,1)S(1)}, bf16[32,1,128,128]{3,2,1,0:T(8,128)(2,1)}, u32[]{:S(2)}) copy-start(bf16[32,1,128,128]{3,2,1,0:T(8,128)(2,1)} %copy-done.8) | copy-start | bytes 3145732
  162.0 3.5 copy-start.3
  162.0 3.7 copy-start.5
  165.8 0.8 copy-start.12
  166.6 1.9 copy-start.18
  199.3 9.0 %slice-start = ((s8[6291456]{0:T(1024)(128)(4,1)}), s8[4194304]{0:T(1024)(128)(4,1)S(1)}, s32[]{:S(2)}) async-start(s8[6291456]{0:T(1024)(128)(4,1)} %bitcast.193), calls=%async_computation.6 | async-start | bytes 8388608
  199.3 9.0 %slice-start.1 = ((s8[6291456]{0:T(1024)(128)(4,1)}), s8[2097152]{0:T(1024)(128)(4,1)S(1)}, s32[]{:S(2)}) async-start(s8[6291456]{0:T(1024)(128)(4,1)} %bitcast.193), calls=%async_computation.7 | async-start | bytes 4194304
  199.3 9.0 %copy-start.19 = (s32[4096]{0:T(1024)S(1)}, s32[4096]{0:T(1024)}, u32[]{:S(2)}) copy-start(s32[4096]{0:T(1024)} %get-tuple-element.46) | copy-start | bytes 49156
  221.4 10.2 %copy-start.14 = (f32[2,2,64,128]{3,2,1,0:T(8,128)S(1)}, f32[2,2,64,128]{3,2,1,0:T(8,128)}, u32[]{:S(2)}) copy-start(f32[2,2,64,128]{3,2,1,0:T(8,128)} %param.9) | copy-start | bytes 393220
  221.4 10.2 %copy-start.15 = (f32[2,2,64,128]{3,2,1,0:T(8,128)S(1)}, f32[2,2,64,128]{3,2,1,0:T(8,128)}, u32[]{:S(2)}) copy-start(f32[2,2,64,128]{3,2,1,0:T(8,128)} %param.10) | copy-start | bytes 393220
  221.5 8.4 %collective-permute-start.2 = (bf16[2,3,64,128]{3,2,1,0:T(8,128)(2,1)S(1)}, bf16[2,3,64,128]{3,2,1,0:T(8,128)(2,1)S(1)}, u32[]{:S(2)}, u32[]{:S(2)}) collective-permute-start(bf16[2,3,64,128]{3,2,1,0:T(8,128)(2,1)S(1)} %get-tuple-element.27), channel_id=1, source_target_pairs={{0,1},{1,2},{2,3},{3,4},{4,5},{5,6},{6,7},{7,8},{8,9},{9,10},{10,1... | collective-permute-start | bytes 294920 | tf_op jit(solution)/shard_map/ppermute | solution.py:15
  225.4 6.1 %collective-permute-start.3 = (bf16[2,3,64,128]{3,2,1,0:T(8,128)(2,1)S(1)}, bf16[2,3,64,128]{3,2,1,0:T(8,128)(2,1)S(1)}, u32[]{:S(2)}, u32[]{:S(2)}) collective-permute-start(bf16[2,3,64,128]{3,2,1,0:T(8,128)(2,1)S(1)} %get-tuple-element.28), channel_id=1, source_target_pairs={{0,2},{1,3},{2,4},{3,5},{4,6},{5,7},{6,8},{7,9},{8,10},{9,11},{10,... | collective-permute-start | bytes 294920 | tf_op jit(solution)/shard_map/ppermute | solution.py:15
  232.6 171.1 %copy-start.17 = (f32[2,2,64,128]{3,2,1,0:T(8,128)}, f32[2,2,64,128]{3,2,1,0:T(8,128)S(1)}, u32[]{:S(2)}) copy-start(f32[2,2,64,128]{3,2,1,0:T(8,128)S(1)} %get-tuple-element.51) | copy-start | bytes 393220
  272.2 247.7 %all-gather.2.cloned.1.call-start = ((), (), s32[]{:S(2)}) async-start(), calls=%async_computation.5 | async-start | bytes 9437184 | tf_op jit(solution)/shard_map/all_gather | solution.py:243
  387.6 10.8 %collective-permute-start.4 = (f32[2,64,1,128]{3,2,1,0:T(1,128)S(1)}, f32[2,64,1,128]{3,2,1,0:T(1,128)S(1)}, u32[]{:S(2)}, u32[]{:S(2)}) collective-permute-start(f32[2,64,1,128]{3,2,1,0:T(1,128)S(1)} %get-tuple-element.19), channel_id=1, source_target_pairs={{0,16},{16,32},{32,48},{48,64},{64,80},{80,96},{96,112},{1,17},{17... | collective-permute-start | bytes 196616 | tf_op jit(solution)/shard_map/ppermute | solution.py:44
  389.7 8.7 %collective-permute-start.5 = (f32[2,64,1,128]{3,2,1,0:T(1,128)S(1)}, f32[2,64,1,128]{3,2,1,0:T(1,128)S(1)}, u32[]{:S(2)}, u32[]{:S(2)}) collective-permute-start(f32[2,64,1,128]{3,2,1,0:T(1,128)S(1)} %get-tuple-element.20), channel_id=1, source_target_pairs={{16,0},{32,16},{48,32},{64,48},{80,64},{96,80},{112,96},{17,1},{33... | collective-permute-start | bytes 196616 | tf_op jit(solution)/shard_map/ppermute | solution.py:45
  391.0 6.5 %collective-permute-start.6 = (f32[2,1,16,128]{3,2,1,0:T(8,128)S(1)}, f32[2,1,16,128]{3,2,1,0:T(8,128)S(1)}, u32[]{:S(2)}, u32[]{:S(2)}) collective-permute-start(f32[2,1,16,128]{3,2,1,0:T(8,128)S(1)} %get-tuple-element.22), channel_id=1, source_target_pairs={{1,0},{2,1},{3,2},{4,3},{5,4},{6,5},{7,6},{8,7},{9,8},{10,9},{11,1... | collective-permute-start | bytes 49160 | tf_op jit(solution)/shard_map/ppermute | solution.py:45
  394.5 3.9 collective-permute-start.7
  400.9 2.9 copy-start.16
Sparse Core Ops, SparseCore 0:
  28.5 64.9 reduce-scatter.2
  272.3 113.3 reduce-scatter.4
  403.9 116.0 all-gather.1
where the time goes:
time: 539 us; the launch traced here: 535 us
  waiting for transfers between devices  231 us (43%)
  local copies, waits for them, and re-layouts  158 us (29%)
  matrix products  44.5 us (8%)
  other arithmetic  38.5 us (7%)
  starting transfers between devices  23.2 us (4%)
  blocking collectives  23.1 us (4%)
  between operations  16 us (3%)
    all_gather x1, waiting for transfers between devices, per_device(): volume_new = lax.all_gather(share_new, 'view', axis=2, tiled=True)  115 us
    reduce_scatter x1, waiting for transfers between devices, per_device(): lax.psum_scatter(grad_part, 'view', scatter_dimension=2, tiled=True)  113 us
    unnamed x53, local copies, waits for them, and re-layouts  34 us
    all_to_all x1, blocking collectives, from_everyone(): lax.all_to_all(jnp.broadcast_to(array[None], (devices, *array.shape)), ax...  23.1 us
    slice x2, local copies, waits for them, and re-layouts, batch_update(): obj_im = windows[:, 1]  17.2 us
    transpose x2, local copies, waits for them, and re-layouts, batch_update(): columns_done = columns_done.reshape(num_slots, 2, num_cols, num_rows).tra...  16 us
    gather x2, local copies, waits for them, and re-layouts, per_device(): lax.dynamic_slice_in_dim(view_reach, offset_col, patch_cols, 1)  14.2 us
    another operation x3, local copies, waits for them, and re-layouts, batch_update(): jnp.stack([probe_re * diff_re + probe_im * diff_im, probe_re * diff_im -...  13.9 us
  transfers between devices with their start and end apart: 11, of which 4 were waited for; matrix products, arithmetic and copies ran while one was open for 38% of the time, Pallas kernels for 0%

commit v1 on v0

v1 whole, which is shorter than its diff:
```python
import functools

import jax
import jax.numpy as jnp
import numpy as np
from jax import lax
from jax.experimental import pallas as pl
from jax.experimental.pallas import tpu as pltpu
from jax.sharding import PartitionSpec as P

rho_weight = 0.5
step_size = 0.5
prior_weight = 0.5
MESH = pl.DeviceIdType.MESH
BATCH = 4
MIB = 2**20


def dft_tables(order):
    counter = np.arange(order)
    angles = ((counter[:, None] * counter[None, :]) % order).astype(np.float32)
    angles = angles * np.float32(2.0 * np.pi / order)
    scaling = np.float32(1.0 / np.sqrt(np.float32(order)))
    re, im = np.cos(angles) * scaling, -np.sin(angles) * scaling
    minus = np.block([[re, -im], [im, re]])
    plus = np.block([[re, im], [-im, re]])
    return jnp.asarray(minus, jnp.bfloat16), jnp.asarray(plus, jnp.bfloat16)


def phi(d):
    return d * lax.rsqrt(1.0 + d * d)


def flag(condition):
    return jnp.where(condition, jnp.float32(1.0), jnp.float32(0.0))


def dot(a, b):
    return jnp.dot(a, b, preferred_element_type=jnp.float32)


def front_kernel(
    nv,
    nt,
    positions,
    live_counts,
    footprints,
    object_hbm,
    dual_hbm,
    probe,
    minus,
    plus,
    counts_hbm,
    weights_hbm,
    volume_hbm,
    object_out,
    dual_out,
    gathered,
    dual_v,
    reach,
    counts_v,
    weights_v,
    volume_v,
    weights_in,
    shadow,
    shadow_out,
    shadow_in,
    patch_tmp,
    power_tmp,
    acc,
    upd_out,
    upd_in,
    resid_full,
    rt,
    grad,
    half,
    halo_out,
    halo_in,
    share,
    local_sem,
    chunk_sem,
    w_send,
    w_recv,
    obj_send,
    obj_recv,
    sh_send,
    sh_recv,
    upd_send,
    upd_recv,
    res_send,
    res_recv,
    rel_send,
    rel_recv,
    rt_send,
    rt_recv,
    halo_send,
    halo_recv,
    ag_send,
    ag_recv,
    ag_local,
):
    v = lax.axis_index("view")
    t = lax.axis_index("tile")
    views, slots = positions.shape
    cols = reach.shape[2] // 3
    depth = volume_hbm.shape[2]
    share_cols = cols // nv
    span = share_cols * depth
    rows = probe.shape[2]
    pw = probe.shape[1]

    def remote(src, dst, send, recv, view, tile):
        return pltpu.make_async_remote_copy(
            src_ref=src,
            dst_ref=dst,
            send_sem=send,
            recv_sem=recv,
            device_id={"view": view, "tile": tile},
            device_id_type=MESH,
        )

    def view_at(k):
        return lax.rem(v + k + nv, nv)

    def tile_at(k):
        return lax.rem(t + k + nt, nt)

    back_v, back_t = view_at(-1), jnp.where(v == 0, tile_at(-1), t)
    fore_v, fore_t = view_at(1), jnp.where(v == nv - 1, tile_at(1), t)

    loads = [
        pltpu.make_async_copy(object_hbm, reach.at[:, :, pl.ds(0, cols), :], local_sem.at[0]),
        pltpu.make_async_copy(dual_hbm, dual_v, local_sem.at[1]),
    ]
    for a in range(views):
        loads.append(
            pltpu.make_async_copy(counts_hbm.at[a], counts_v.at[a], local_sem.at[2 + a])
        )

    def chunk_copies(c):
        first = pl.multiple_of(c * span, span)
        return (
            pltpu.make_async_copy(
                weights_hbm.at[:, :, pl.ds(first, span)],
                weights_v.at[:, :, pl.ds(first, span)],
                chunk_sem.at[0, c],
            ),
            pltpu.make_async_copy(
                volume_hbm.at[:, pl.ds(c * share_cols, share_cols)],
                volume_v.at[:, pl.ds(c * share_cols, share_cols)],
                chunk_sem.at[1, c],
            ),
        )

    loads[0].start()
    for c in range(nv):
        for copy in chunk_copies(c):
            copy.start()
    for copy in loads[1:]:
        copy.start()

    barrier = pltpu.get_barrier_semaphore()

    def greet(view, tile):
        pl.semaphore_signal(
            barrier, inc=1, device_id={"view": view, "tile": tile}, device_id_type=MESH
        )

    for k in range(1, nv):
        greet(view_at(k), t)
    for k in range(1, nt):
        greet(v, tile_at(k))
    greet(back_v, back_t)
    greet(fore_v, fore_t)
    pl.semaphore_wait(barrier, nv + nt)

    object_copies = [
        remote(
            object_hbm,
            reach.at[:, :, pl.ds(k * cols, cols), :],
            obj_send.at[k - 1],
            obj_recv.at[k - 1],
            v,
            tile_at(-k),
        )
        for k in (1, 2)
    ]
    for copy in object_copies:
        copy.start()

    weight_copies = []
    for k in range(1, nv):
        to = view_at(k)
        copy = remote(
            weights_hbm.at[:, :, pl.ds(pl.multiple_of(to * span, span), span)],
            weights_in.at[k - 1],
            w_send.at[k - 1],
            w_recv.at[k - 1],
            to,
            t,
        )
        copy.start()
        weight_copies.append(copy)

    shadow[...] = jnp.zeros_like(shadow)

    def project(c, _):
        for copy in chunk_copies(c):
            copy.wait()
        first = pl.multiple_of(c * span, span)
        left = weights_v[:, :, pl.ds(first, span)].reshape(views * 2 * cols, span)
        block = volume_v[:, pl.ds(c * share_cols, share_cols)].astype(jnp.bfloat16)
        right = jnp.concatenate(
            [block[0].reshape(span, rows), block[1].reshape(span, rows)], axis=1
        )
        shadow[...] += dot(left, right)
        return 0

    lax.fori_loop(0, nv, project, 0)

    foot = [footprints[a, 0] for a in range(views)]

    def shadow_part(a, k, part):
        first = a * 2 * cols + part * cols
        return shadow[first : first + cols, k * rows : (k + 1) * rows]

    def placed(to, a, k):
        return shadow_part(a, k, 0) * flag(foot[a] == to) + shadow_part(a, k, 1) * flag(
            foot[a] + 1 == to
        )

    shadow_copies = []
    for step in range(1, nt):
        to = tile_at(step)
        for a in range(views):
            for k in range(2):
                shadow_out[step - 1, a, k] = placed(to, a, k).astype(jnp.bfloat16)
        copy = remote(
            shadow_out.at[step - 1],
            shadow_in.at[step - 1],
            sh_send.at[step - 1],
            sh_recv.at[step - 1],
            v,
            to,
        )
        copy.start()
        shadow_copies.append(copy)

    probe_re, probe_im = probe[0], probe[1]
    acc[...] = jnp.zeros_like(acc)
    patch_tmp[...] = jnp.zeros_like(patch_tmp)
    power_tmp[...] = jnp.zeros_like(power_tmp)
    power_tmp[cols : cols + pw, :] = probe_re * probe_re + probe_im * probe_im
    for copy in loads[:2]:
        copy.wait()
    for copy in object_copies:
        copy.wait()
    for k in (1, 2):
        inside = flag(t + k < nt)
        for a in range(views):
            for plane in range(2):
                reach[a, plane, k * cols : (k + 1) * cols, :] = (
                    reach[a, plane, k * cols : (k + 1) * cols, :] * inside
                )

    def patches(a, b):
        base = b * BATCH
        offsets = [positions[a, base + j] for j in range(BATCH)]
        live_count = live_counts[a, 0]
        lives = [flag(base + j < live_count) for j in range(BATCH)]
        re, im = probe[0], probe[1]
        exits = []
        for j in range(BATCH):
            obj_re = reach[a, 0, pl.ds(offsets[j], pw), :]
            obj_im = reach[a, 1, pl.ds(offsets[j], pw), :]
            exits.append(
                jnp.concatenate(
                    [re * obj_re - im * obj_im, re * obj_im + im * obj_re], axis=0
                ).astype(jnp.bfloat16)
            )
        done = dot(minus[...], jnp.concatenate(exits, axis=1)).astype(jnp.bfloat16)
        done = jnp.concatenate(
            [
                jnp.concatenate(
                    [
                        done[:pw, j * rows : (j + 1) * rows],
                        done[pw:, j * rows : (j + 1) * rows],
                    ],
                    axis=1,
                )
                for j in range(BATCH)
            ],
            axis=0,
        )
        spectrum = dot(done, plus[...])
        s_re, s_im = spectrum[:, :rows], spectrum[:, rows:]
        counts = counts_v[a, pl.ds(base, BATCH)].astype(jnp.float32).reshape(BATCH * pw, rows)
        power = 256.0 * (s_re * s_re + s_im * s_im) + 64.0
        factor = counts * lax.rsqrt(jnp.maximum(counts * power, 1e-20))
        replaced = jnp.concatenate([s_re * factor, s_im * factor], axis=1).astype(jnp.bfloat16)
        inverse = dot(replaced, minus[...]).astype(jnp.bfloat16)
        inverse = jnp.concatenate(
            [
                jnp.concatenate(
                    [
                        inverse[j * pw : (j + 1) * pw, :rows],
                        inverse[j * pw : (j + 1) * pw, rows:],
                    ],
                    axis=0,
                )
                for j in range(BATCH)
            ],
            axis=1,
        )
        wave = dot(plus[...], inverse)
        for j in range(BATCH):
            diff = wave[:, j * rows : (j + 1) * rows] - exits[j].astype(jnp.float32)
            d_re, d_im = diff[:pw] * lives[j], diff[pw:] * lives[j]
            patch_tmp[j, 0, cols : cols + pw, :] = re * d_re + im * d_im
            patch_tmp[j, 1, cols : cols + pw, :] = re * d_im - im * d_re
        for plane in range(2):
            total = acc[a, plane]
            for j in range(BATCH):
                total = total + patch_tmp[j, plane, pl.ds(cols - offsets[j], 3 * cols), :]
            acc[a, plane] = total
        total = acc[a, 2]
        for j in range(BATCH):
            total = total + power_tmp[pl.ds(cols - offsets[j], 3 * cols), :] * lives[j]
        acc[a, 2] = total

    update_copies = []
    for a in range(views):
        loads[2 + a].wait()
        lax.fori_loop(0, slots // BATCH, lambda b, _, a=a: (patches(a, b), 0)[1], 0)
        for k in (1, 2):
            upd_out[a, k - 1] = acc[a, :, k * cols : (k + 1) * cols, :].astype(jnp.bfloat16)
            copy = remote(
                upd_out.at[a, k - 1],
                upd_in.at[a, k - 1],
                upd_send.at[a, k - 1],
                upd_recv.at[a, k - 1],
                v,
                tile_at(k),
            )
            copy.start()
            update_copies.append(copy)

    for copy in shadow_copies:
        copy.wait()
    for copy in update_copies:
        copy.wait()
    from_one, from_two = flag(t >= 1), flag(t >= 2)
    for a in range(views):
        upd = (
            acc[a, :, :cols, :]
            + upd_in[a, 0].astype(jnp.float32) * from_one
            + upd_in[a, 1].astype(jnp.float32) * from_two
        )
        scale = 1.0 / (1.0 + upd[2])
        for k in range(2):
            projection = placed(t, a, k)
            for step in range(1, nt):
                projection = projection + shadow_in[step - 1, a, k].astype(jnp.float32)
            obj = reach[a, k, :cols, :]
            dual = dual_v[a, k]
            new = obj + upd[k] * scale - rho_weight * (obj - projection - dual)
            object_out[a, k] = new
            dual_new = dual + projection - new
            dual_out[a, k] = dual_new
            resid_full[t, a, k] = dual_new.astype(jnp.bfloat16)

    core = lax.rem(t, 2)
    sibling = t + 1 - 2 * core
    chips = nt // 2
    resid_copies = [
        remote(
            resid_full.at[t],
            resid_full.at[t],
            res_send.at[m],
            res_recv.at[m],
            v,
            tile_at(2 * m) if m else sibling,
        )
        for m in range(chips)
    ]
    for copy in resid_copies[1:]:
        copy.start()
    resid_copies[0].start()
    relays = []
    for m in range(1, chips):
        source = tile_at(-2 * m)
        remote(
            resid_full.at[source],
            resid_full.at[source],
            res_send.at[m],
            res_recv.at[m],
            v,
            source,
        ).wait_recv()
        relay = remote(
            resid_full.at[source],
            resid_full.at[source],
            rel_send.at[m - 1],
            rel_recv.at[m - 1],
            v,
            sibling,
        )
        relay.start()
        relays.append(relay)
    remote(
        resid_full.at[sibling], resid_full.at[sibling], res_send.at[0], res_recv.at[0], v, sibling
    ).wait_recv()
    for m in range(1, chips):
        source = lax.rem(sibling - 2 * m + nt, nt)
        remote(
            resid_full.at[source],
            resid_full.at[source],
            rel_send.at[m - 1],
            rel_recv.at[m - 1],
            v,
            sibling,
        ).wait_recv()
    for copy in resid_copies + relays:
        copy.wait_send()

    for a in range(views):
        for k in range(2):
            window = jnp.concatenate([resid_full[foot[a], a, k], resid_full[foot[a] + 1, a, k]], axis=0)
            rt[0, k * rows : (k + 1) * rows, a * 2 * cols : (a + 1) * 2 * cols] = (
                window.astype(jnp.float32).T.astype(jnp.bfloat16)
            )
    rt_copies = []
    for k in range(1, nv):
        copy = remote(rt.at[0], rt.at[k], rt_send.at[k - 1], rt_recv.at[k - 1], view_at(k), t)
        copy.start()
        rt_copies.append(copy)

    own = weights_v[:, :, pl.ds(pl.multiple_of(v * span, span), span)]
    grad[...] = dot(rt[0], own.reshape(views * 2 * cols, span))
    for k in range(1, nv):
        weight_copies[k - 1].wait()
        rt_copies[k - 1].wait()
        grad[...] += dot(rt[k], weights_in[k - 1].reshape(views * 2 * cols, span))

    for c in range(share_cols):
        for k in range(2):
            part = grad[k * rows : (k + 1) * rows, c * depth : (c + 1) * depth].T
            half[k, c] = volume_v[k, v * share_cols + c] - step_size * part

    for k in range(2):
        halo_out[0, k] = half[k, 0].astype(jnp.bfloat16)
        halo_out[1, k] = half[k, share_cols - 1].astype(jnp.bfloat16)
    halo_copies = [
        remote(halo_out.at[0], halo_in.at[1], halo_send.at[0], halo_recv.at[1], back_v, back_t),
        remote(halo_out.at[1], halo_in.at[0], halo_send.at[1], halo_recv.at[0], fore_v, fore_t),
    ]
    for copy in halo_copies:
        copy.start()

    row = lax.broadcasted_iota(jnp.int32, (depth, rows), 0)
    lane = lax.broadcasted_iota(jnp.int32, (depth, rows), 1)

    def inner(x):
        below = jnp.where(row == 0, 0.0, pltpu.roll(x, 1, 0))
        above = jnp.where(row == depth - 1, 0.0, pltpu.roll(x, depth - 1, 0))
        left = jnp.where(lane == 0, 0.0, pltpu.roll(x, 1, 1))
        right = jnp.where(lane == rows - 1, 0.0, pltpu.roll(x, rows - 1, 1))
        return phi(x - below) + phi(x - above) + phi(x - left) + phi(x - right)

    def finish(k, c, before, after):
        x = half[k, c]
        prior = inner(x) + phi(x - before) + phi(x - after)
        share[k, c] = (x - (step_size * prior_weight) * prior).astype(jnp.bfloat16)

    for k in range(2):
        lax.fori_loop(
            1,
            share_cols - 1,
            lambda c, _, k=k: (finish(k, c, half[k, c - 1], half[k, c + 1]), 0)[1],
            0,
        )
    for copy in halo_copies:
        copy.wait()
    has_back = flag((v > 0) | (t > 0))
    has_fore = flag((v < nv - 1) | (t < nt - 1))
    for k in range(2):
        finish(k, 0, halo_in[0, k].astype(jnp.float32) * has_back, half[k, 1])
        finish(
            k,
            share_cols - 1,
            half[k, share_cols - 2],
            halo_in[1, k].astype(jnp.float32) * has_fore,
        )

    ag_copies = []
    for k in range(1, nv):
        copy = remote(
            share, gathered.at[v], ag_send.at[k - 1], ag_recv.at[k - 1], view_at(k), t
        )
        copy.start()
        ag_copies.append(copy)
    own_copy = pltpu.make_async_copy(share, gathered.at[v], ag_local)
    own_copy.start()
    for k in range(1, nv):
        source = view_at(-k)
        remote(
            share, gathered.at[source], ag_send.at[k - 1], ag_recv.at[k - 1], source, t
        ).wait_recv()
    for copy in ag_copies:
        copy.wait_send()
    own_copy.wait()


def widen_kernel(x_ref, o_ref):
    o_ref[...] = x_ref[0].astype(jnp.float32)


def per_device(
    nv,
    nt,
    object_band,
    dual_band,
    probe_field,
    positions,
    live_counts,
    photon_counts,
    footprints,
    weights,
    volume,
):
    views, _, cols, rows = object_band.shape
    pw = probe_field.shape[1]
    slots = positions.shape[1]
    depth = volume.shape[2]
    share_cols = cols // nv
    span = share_cols * depth
    minus, plus = dft_tables(pw)
    any_space = pl.BlockSpec(memory_space=pl.ANY)
    smem = pl.BlockSpec(memory_space=pltpu.SMEM)
    vmem = pl.BlockSpec(memory_space=pltpu.VMEM)
    bf16, f32 = jnp.bfloat16, jnp.float32
    dma = pltpu.SemaphoreType.DMA
    chips = nt // 2
    band = jax.ShapeDtypeStruct(object_band.shape, f32)
    object_new, dual_new, gathered = pl.pallas_call(
        functools.partial(front_kernel, nv, nt),
        out_shape=(
            band,
            band,
            jax.ShapeDtypeStruct((nv, 2, share_cols, depth, rows), bf16),
        ),
        in_specs=[smem] * 3 + [any_space] * 2 + [vmem] * 3 + [any_space] * 3,
        out_specs=(vmem, vmem, any_space),
        scratch_shapes=[
            pltpu.VMEM((views, 2, cols, rows), f32),
            pltpu.VMEM((views, 2, 3 * cols, rows), f32),
            pltpu.VMEM((views, slots, pw, rows), jnp.int32),
            pltpu.VMEM(weights.shape, bf16),
            pltpu.VMEM(volume.shape, f32),
            pltpu.VMEM((nv - 1, views, 2 * cols, span), bf16),
            pltpu.VMEM((views * 2 * cols, 2 * rows), f32),
            pltpu.VMEM((nt - 1, views, 2, cols, rows), bf16),
            pltpu.VMEM((nt - 1, views, 2, cols, rows), bf16),
            pltpu.VMEM((BATCH, 2, 4 * cols, rows), f32),
            pltpu.VMEM((4 * cols, rows), f32),
            pltpu.VMEM((views, 3, 3 * cols, rows), f32),
            pltpu.VMEM((views, 2, 3, cols, rows), bf16),
            pltpu.VMEM((views, 2, 3, cols, rows), bf16),
            pltpu.VMEM((nt, views, 2, cols, rows), bf16),
            pltpu.VMEM((nv, 2 * rows, views * 2 * cols), bf16),
            pltpu.VMEM((2 * rows, span), f32),
            pltpu.VMEM((2, share_cols, depth, rows), f32),
            pltpu.VMEM((2, 2, depth, rows), bf16),
            pltpu.VMEM((2, 2, depth, rows), bf16),
            pltpu.VMEM((2, share_cols, depth, rows), bf16),
            dma((2 + views,)),
            dma((2, nv)),
            dma((nv - 1,)),
            dma((nv - 1,)),
            dma((2,)),
            dma((2,)),
            dma((nt - 1,)),
            dma((nt - 1,)),
            dma((views, 2)),
            dma((views, 2)),
            dma((chips,)),
            dma((chips,)),
            dma((chips - 1,)),
            dma((chips - 1,)),
            dma((nv - 1,)),
            dma((nv - 1,)),
            dma((2,)),
            dma((2,)),
            dma((nv - 1,)),
            dma((nv - 1,)),
            dma(()),
        ],
        compiler_params=pltpu.CompilerParams(
            collective_id=0, has_side_effects=True, vmem_limit_bytes=52 * MIB
        ),
        name="front",
    )(
        positions,
        live_counts,
        footprints,
        object_band,
        dual_band,
        probe_field,
        minus,
        plus,
        photon_counts,
        weights,
        volume,
    )
    volume_new = pl.pallas_call(
        widen_kernel,
        grid=(nv,),
        out_shape=jax.ShapeDtypeStruct(volume.shape, f32),
        in_specs=[pl.BlockSpec((1, 2, share_cols, depth, rows), lambda i: (i, 0, 0, 0, 0))],
        out_specs=pl.BlockSpec((2, share_cols, depth, rows), lambda i: (0, i, 0, 0)),
        compiler_params=pltpu.CompilerParams(vmem_limit_bytes=32 * MIB),
        name="widen",
    )(gathered)
    return object_new, dual_new, volume_new


def solution(mesh):
    return jax.shard_map(
        functools.partial(per_device, mesh.shape["view"], mesh.shape["tile"]),
        mesh=mesh,
        in_specs=(
            P("view", None, "tile", None),
            P("view", None, "tile", None),
            P(),
            P("view", "tile"),
            P("view", "tile"),
            P("view", "tile", None, None),
            P("view", "tile"),
            P("view", None, "tile"),
            P(None, "tile", None, None),
        ),
        out_specs=(
            P("view", None, "tile", None),
            P("view", None, "tile", None),
            P(None, "tile", None, None),
        ),
        check_vma=False,
    )
```

time: 539 us -> 173 us (0.32)
  waiting for transfers between devices: 231 us -> 0 us
  Pallas kernels: 0 us -> 162 us
  local copies, waits for them, and re-layouts: 158 us -> 10.2 us
  matrix products: 44.5 us -> 0 us
  other arithmetic: 38.5 us -> 0 us
  starting transfers between devices: 23.2 us -> 0 us
  blocking collectives: 23.1 us -> 0 us
  between operations: 16 us -> 0.65 us
    pallas_call x0 -> x2, Pallas kernels: none -> 162 us  [the longest x1 157 us: per_device(): pl.pallas_call(functools.partial(front_kernel, nv, nt), out_shape=(band,...]
    all_gather x1 -> x0, waiting for transfers between devices: 115 us -> none  [per_device(): volume_new = lax.all_gather(share_new, 'view', axis=2, tiled=True)]
    reduce_scatter x2 -> x0, waiting for transfers between devices: 114 us -> none  [the longest x1 113 us: per_device(): lax.psum_scatter(grad_part, 'view', scatter_dimension=2, tiled=True)]
    dot_general x12 -> x0, matrix products: 44.5 us -> none  [the longest x2 13.1 us: per_device(): jnp.dot(placement.T, flat, precision=lax.Precision.HIGHEST, preferred_ele...]
    transpose x6 -> x0, local copies, waits for them, and re-layouts: 40.8 us -> none  [the longest x2 16 us: batch_update(): columns_done = columns_done.reshape(num_slots, 2, num_cols, num_rows).tra...]
    reshape x9 -> x0, local copies, waits for them, and re-layouts: 33.9 us -> none  [the longest x1 8.91 us: per_device(): grad_part = jnp.einsum('acx,akch->kxh', weights, residual_windows, prefer...]
    unnamed x53 -> x18, local copies, waits for them, and re-layouts: 34 us -> 10.2 us
    all_to_all x1 -> x0, blocking collectives: 23.1 us -> none  [from_everyone(): lax.all_to_all(jnp.broadcast_to(array[None], (devices, *array.shape)), ax...]
  transfers between devices with their start and end apart: 11 -> 0, of which waited for: 4 -> 0; matrix products, arithmetic and copies ran while one was open for 38% -> 0% of each run, Pallas kernels for 0% -> 0%
where the time goes in v1:
time: 173 us; the launch traced here: 172 us
  Pallas kernels  162 us (94%)
  local copies, waits for them, and re-layouts  10.2 us (6%)
    pallas_call x1, Pallas kernels, per_device(): pl.pallas_call(functools.partial(front_kernel, nv, nt), out_shape=(band,...  157 us
    unnamed x18, local copies, waits for them, and re-layouts  10.2 us
    pallas_call x1, Pallas kernels, per_device(): pl.pallas_call(widen_kernel, grid=(nv,), out_shape=jax.ShapeDtypeStruct(v...  4.49 us

profile of v1, /device:TPU:1, one launch (start us, length us, event | category | flops | bytes accessed | tf_op | source)
XLA Modules:
  0.0 172.4 jit_solution(2690971591472862433)
XLA Ops:
  0.6 0.7 copy.14.live_counts
  1.4 0.7 copy.15.footprints
  2.1 0.0 copy-start.1
  2.1 0.9 copy-done.1
  3.0 0.0 copy-start.2
  3.0 0.9 copy-done.2
  3.9 0.0 copy-start.3
  3.9 0.9 copy-done.3
  4.8 0.0 copy-start.4
  4.8 0.9 copy-done.4
  5.7 0.0 copy-start.5
  5.7 0.9 copy-done.5
  6.6 0.0 copy-start.6
  6.6 0.7 copy-done.6
  7.3 157.1 %front.1 = (f32[2,2,64,128]{3,2,1,0:T(8,128)S(1)}, f32[2,2,64,128]{3,2,1,0:T(8,128)S(1)}, bf16[8,2,8,128,128]{4,3,2,1,0:T(8,128)(2,1)}) custom-call(s32[2,32]{1,0:T(2,128)S(1)} %copy-done.6, s32[2,1]{1,0:T(2,128)S(1)} %copy.14.live_counts, s32[2,1]{1,0:T(2,128)S(1)} %copy.15.footprints, f32[2,2,64,128]{3,2,1,0:T(8,128)S(1)} %copy-done.1, ...), custom_call_target="tpu_custom_call" | custom-call | tf_op jit(solution)/shard_map/front/pallas_call | solution.py:545
  164.4 0.0 copy-start
  164.4 2.2 %copy-done = bf16[8,2,8,128,128]{4,3,2,1,0:T(8,128)(2,1)S(1)} copy-done((bf16[8,2,8,128,128]{4,3,2,1,0:T(8,128)(2,1)S(1)}, bf16[8,2,8,128,128]{4,3,2,1,0:T(8,128)(2,1)}, u32[]{:S(2)}) %copy-start) | copy-done | bytes 4194328
  166.6 4.5 %widen.1 = f32[2,64,128,128]{3,2,1,0:T(8,128)} custom-call(bf16[8,2,8,128,128]{4,3,2,1,0:T(8,128)(2,1)S(1)} %copy-done), custom_call_target="tpu_custom_call" | custom-call | tf_op jit(solution)/shard_map/widen/pallas_call | solution.py:615
  171.1 0.7 copy.18
  171.8 0.7 copy.19
Async XLA Ops:
  2.1 0.9 copy-start.1
  3.0 0.9 copy-start.2
  3.9 0.9 copy-start.3
  4.8 0.9 copy-start.4
  5.7 0.9 copy-start.5
  6.6 0.7 copy-start.6
  164.4 2.2 %copy-start = (bf16[8,2,8,128,128]{4,3,2,1,0:T(8,128)(2,1)S(1)}, bf16[8,2,8,128,128]{4,3,2,1,0:T(8,128)(2,1)}, u32[]{:S(2)}) copy-start(bf16[8,2,8,128,128]{4,3,2,1,0:T(8,128)(2,1)} %get-tuple-element.8.x_ref) | copy-start | bytes 12582916

commit v2 on v1

--- a/solution.py
+++ b/solution.py
@@ -13,6 +13,9 @@
 prior_weight = 0.5
 MESH = pl.DeviceIdType.MESH
 BATCH = 4
+FRONT_VMEM = 60
+WIDEN_VMEM = 60
+PUMP = (11, 4, 2, 4, 4, 4, 4, 4)
 MIB = 2**20
 
 
@@ -47,15 +50,18 @@
     footprints,
     object_hbm,
     dual_hbm,
-    probe,
-    minus,
-    plus,
+    probe_hbm,
+    minus_hbm,
+    plus_hbm,
     counts_hbm,
     weights_hbm,
     volume_hbm,
     object_out,
     dual_out,
     gathered,
+    probe,
+    minus,
+    plus,
     dual_v,
     reach,
     counts_v,
@@ -65,12 +71,15 @@
     shadow,
     shadow_out,
     shadow_in,
+    shared_out,
+    shared_in,
     patch_tmp,
     power_tmp,
     acc,
     upd_out,
     upd_in,
-    resid_full,
+    resid_first,
+    resid_second,
     rt,
     grad,
     half,
@@ -85,6 +94,8 @@
     obj_recv,
     sh_send,
     sh_recv,
+    gr_send,
+    gr_recv,
     upd_send,
     upd_recv,
     res_send,
@@ -97,11 +108,11 @@
     halo_recv,
     ag_send,
     ag_recv,
-    ag_local,
 ):
     v = lax.axis_index("view")
     t = lax.axis_index("tile")
     views, slots = positions.shape
+    resid_full = (resid_first, resid_second)
     cols = reach.shape[2] // 3
     depth = volume_hbm.shape[2]
     share_cols = cols // nv
@@ -125,6 +136,18 @@
     def tile_at(k):
         return lax.rem(t + k + nt, nt)
 
+    group = 4
+    levels = nt // group
+    z, place = t // group, lax.rem(t, group)
+    core = lax.rem(t, 2)
+    sibling = t + 1 - 2 * core
+    beside = t + 2 - 4 * (place // 2)
+    view_x = lax.rem(v, 2)
+    over = v + 1 - 2 * view_x
+
+    def level_at(k):
+        return lax.rem(z + k + levels, levels)
+
     back_v, back_t = view_at(-1), jnp.where(v == 0, tile_at(-1), t)
     fore_v, fore_t = view_at(1), jnp.where(v == nv - 1, tile_at(1), t)
 
@@ -136,6 +159,10 @@
         loads.append(
             pltpu.make_async_copy(counts_hbm.at[a], counts_v.at[a], local_sem.at[2 + a])
         )
+    for i, (source, target) in enumerate(
+        ((probe_hbm, probe), (minus_hbm, minus), (plus_hbm, plus))
+    ):
+        loads.append(pltpu.make_async_copy(source, target, local_sem.at[2 + views + i]))
 
     def chunk_copies(c):
         first = pl.multiple_of(c * span, span)
@@ -188,19 +215,38 @@
     for copy in object_copies:
         copy.start()
 
-    weight_copies = []
-    for k in range(1, nv):
-        to = view_at(k)
-        copy = remote(
-            weights_hbm.at[:, :, pl.ds(pl.multiple_of(to * span, span), span)],
-            weights_in.at[k - 1],
-            w_send.at[k - 1],
-            w_recv.at[k - 1],
-            to,
-            t,
-        )
-        copy.start()
-        weight_copies.append(copy)
+    peers = nv - 1
+    piece_rows = 32
+    per_view = 2 * cols // piece_rows
+    pieces = peers * views * per_view
+
+    def pump(first, count):
+        for extra in range(count):
+            index = first + extra
+            k = index % peers
+            row_block = index // peers
+            a = row_block // per_view
+            rows_at = pl.multiple_of((row_block % per_view) * piece_rows, piece_rows)
+            lane = k + 1
+            to = lax.rem(v - view_x + 2 * (lane // 2), nv) + lax.rem(view_x + lane, 2)
+            remote(
+                weights_hbm.at[a, pl.ds(rows_at, piece_rows), pl.ds(pl.multiple_of(to * span, span), span)],
+                weights_in.at[k, a, pl.ds(rows_at, piece_rows), :],
+                w_send.at[k],
+                w_recv.at[k],
+                to,
+                t,
+            ).start()
+
+    pumped = 0
+
+    def pump_some(count):
+        nonlocal pumped
+        count = min(count, pieces - pumped)
+        pump(pumped, count)
+        pumped += count
+
+    pump_some(PUMP[0])
 
     shadow[...] = jnp.zeros_like(shadow)
 
@@ -218,7 +264,7 @@
 
     lax.fori_loop(0, nv, project, 0)
 
-    foot = [footprints[a, 0] for a in range(views)]
+    foot = [footprints[a] for a in range(views)]
 
     def shadow_part(a, k, part):
         first = a * 2 * cols + part * cols
@@ -229,23 +275,56 @@
             foot[a] + 1 == to
         )
 
-    shadow_copies = []
-    for step in range(1, nt):
-        to = tile_at(step)
-        for a in range(views):
-            for k in range(2):
-                shadow_out[step - 1, a, k] = placed(to, a, k).astype(jnp.bfloat16)
-        copy = remote(
-            shadow_out.at[step - 1],
-            shadow_in.at[step - 1],
-            sh_send.at[step - 1],
-            sh_recv.at[step - 1],
+    def level_copy(k):
+        return remote(
+            shadow_out.at[k - 1],
+            shadow_in.at[k - 1],
+            sh_send.at[k - 1],
+            sh_recv.at[k - 1],
             v,
-            to,
-        )
-        copy.start()
-        shadow_copies.append(copy)
-
+            level_at(k) * group + place,
+        )
+
+    def group_copy(k):
+        return remote(
+            shared_out.at[k - 1],
+            shared_in.at[k - 1],
+            gr_send.at[k - 1],
+            gr_recv.at[k - 1],
+            v,
+            z * group + lax.rem(place + k, group),
+        )
+
+    for step in range(1, levels):
+        for k in range(group):
+            to = level_at(step) * group + k
+            for a in range(views):
+                for plane in range(2):
+                    shadow_out[step - 1, k, a, plane] = placed(to, a, plane).astype(jnp.bfloat16)
+        level_copy(step).start()
+
+    def level_sum(to, k, a, plane):
+        total = placed(to, a, plane)
+        for step in range(1, levels):
+            total = total + shadow_in[step - 1, k, a, plane].astype(jnp.float32)
+        return total
+
+    def share_sums():
+        for step in range(1, levels):
+            level_copy(step).wait()
+        for step in range(1, group):
+            k = lax.rem(place + step, group)
+            for a in range(views):
+                for plane in range(2):
+                    shared_out[step - 1, a, plane] = level_sum(
+                        z * group + k, k, a, plane
+                    ).astype(jnp.bfloat16)
+            group_copy(step).start()
+
+    pump_some(PUMP[1])
+
+    for copy in loads[2 + views :]:
+        copy.wait()
     probe_re, probe_im = probe[0], probe[1]
     acc[...] = jnp.zeros_like(acc)
     patch_tmp[...] = jnp.zeros_like(patch_tmp)
@@ -266,7 +345,7 @@
     def patches(a, b):
         base = b * BATCH
         offsets = [positions[a, base + j] for j in range(BATCH)]
-        live_count = live_counts[a, 0]
+        live_count = live_counts[a]
         lives = [flag(base + j < live_count) for j in range(BATCH)]
         re, im = probe[0], probe[1]
         exits = []
@@ -328,29 +407,39 @@
             total = total + power_tmp[pl.ds(cols - offsets[j], 3 * cols), :] * lives[j]
         acc[a, 2] = total
 
-    update_copies = []
-    for a in range(views):
-        loads[2 + a].wait()
-        lax.fori_loop(0, slots // BATCH, lambda b, _, a=a: (patches(a, b), 0)[1], 0)
+    def update_copy(a, k):
+        return remote(
+            upd_out.at[a, k - 1],
+            upd_in.at[a, k - 1],
+            upd_send.at[a, k - 1],
+            upd_recv.at[a, k - 1],
+            v,
+            tile_at(k),
+        )
+
+    def run_patches(a, first, last):
+        nonlocal pumped
+        each = min(PUMP[2], (pieces - pumped) // (last - first))
+        base = pumped
+
+        def body(b, _):
+            pump(base + (b - first) * each, each)
+            patches(a, b)
+            return 0
+
+        lax.fori_loop(first, last, body, 0)
+        pumped += each * (last - first)
+
+    def send_update(a):
         for k in (1, 2):
             upd_out[a, k - 1] = acc[a, :, k * cols : (k + 1) * cols, :].astype(jnp.bfloat16)
-            copy = remote(
-                upd_out.at[a, k - 1],
-                upd_in.at[a, k - 1],
-                upd_send.at[a, k - 1],
-                upd_recv.at[a, k - 1],
-                v,
-                tile_at(k),
-            )
-            copy.start()
-            update_copies.append(copy)
-
-    for copy in shadow_copies:
-        copy.wait()
-    for copy in update_copies:
-        copy.wait()
+            update_copy(a, k).start()
+
     from_one, from_two = flag(t >= 1), flag(t >= 2)
-    for a in range(views):
+
+    def finish_object(a):
+        for k in (1, 2):
+            update_copy(a, k).wait()
         upd = (
             acc[a, :, :cols, :]
             + upd_in[a, 0].astype(jnp.float32) * from_one
@@ -358,89 +447,141 @@
         )
         scale = 1.0 / (1.0 + upd[2])
         for k in range(2):
-            projection = placed(t, a, k)
-            for step in range(1, nt):
-                projection = projection + shadow_in[step - 1, a, k].astype(jnp.float32)
+            projection = level_sum(t, place, a, k)
+            for step in range(1, group):
+                projection = projection + shared_in[step - 1, a, k].astype(jnp.float32)
             obj = reach[a, k, :cols, :]
             dual = dual_v[a, k]
             new = obj + upd[k] * scale - rho_weight * (obj - projection - dual)
             object_out[a, k] = new
             dual_new = dual + projection - new
             dual_out[a, k] = dual_new
-            resid_full[t, a, k] = dual_new.astype(jnp.bfloat16)
-
-    core = lax.rem(t, 2)
-    sibling = t + 1 - 2 * core
-    chips = nt // 2
-    resid_copies = [
-        remote(
-            resid_full.at[t],
-            resid_full.at[t],
-            res_send.at[m],
-            res_recv.at[m],
+            resid_full[a][t, k] = dual_new.astype(jnp.bfloat16)
+
+    def source_at(lane, tile):
+        k, j = lane // 2, lane % 2
+        base = lax.rem(tile // group - k + levels, levels) * group
+        spot = lax.rem(tile, group)
+        return base + (lax.rem(spot + 2, group) if j else spot)
+
+    lanes = 2 * levels
+
+    def resid_copy(a, lane, source, to):
+        return remote(
+            resid_full[a].at[source],
+            resid_full[a].at[source],
+            res_send.at[a, lane],
+            res_recv.at[a, lane],
             v,
-            tile_at(2 * m) if m else sibling,
-        )
-        for m in range(chips)
-    ]
-    for copy in resid_copies[1:]:
-        copy.start()
-    resid_copies[0].start()
-    relays = []
-    for m in range(1, chips):
-        source = tile_at(-2 * m)
-        remote(
-            resid_full.at[source],
-            resid_full.at[source],
-            res_send.at[m],
-            res_recv.at[m],
-            v,
-            source,
-        ).wait_recv()
-        relay = remote(
-            resid_full.at[source],
-            resid_full.at[source],
-            rel_send.at[m - 1],
-            rel_recv.at[m - 1],
+            to,
+        )
+
+    def relay_copy(a, lane, source):
+        return remote(
+            resid_full[a].at[source],
+            resid_full[a].at[source],
+            rel_send.at[a, lane],
+            rel_recv.at[a, lane],
             v,
             sibling,
         )
-        relay.start()
-        relays.append(relay)
-    remote(
-        resid_full.at[sibling], resid_full.at[sibling], res_send.at[0], res_recv.at[0], v, sibling
-    ).wait_recv()
-    for m in range(1, chips):
-        source = lax.rem(sibling - 2 * m + nt, nt)
-        remote(
-            resid_full.at[source],
-            resid_full.at[source],
-            rel_send.at[m - 1],
-            rel_recv.at[m - 1],
-            v,
-            sibling,
-        ).wait_recv()
-    for copy in resid_copies + relays:
-        copy.wait_send()
-
-    for a in range(views):
+
+    def send_resid(a):
+        resid_copy(a, 1, t, beside).start()
+        for k in range(1, levels):
+            resid_copy(a, 2 * k, t, level_at(k) * group + place).start()
+        relay_copy(a, 0, t).start()
+
+    def relay_resid(a):
+        resid_copy(a, 1, beside, beside).wait_recv()
+        for k in range(1, levels):
+            resid_copy(a, 2 * k + 1, beside, level_at(k) * group + place).start()
+        relay_copy(a, 1, beside).start()
+        for lane in range(2, lanes):
+            source = source_at(lane, t)
+            resid_copy(a, lane, source, t).wait_recv()
+            relay_copy(a, lane, source).start()
+
+    def rt_part(k, a):
+        return rt.at[k, :, pl.ds(a * 2 * cols, 2 * cols)]
+
+    def rt_copy(a, lane, k, to):
+        return remote(
+            rt_part(k, a),
+            rt_part(lane, a),
+            rt_send.at[a, lane - 1],
+            rt_recv.at[a, lane - 1],
+            to,
+            t,
+        )
+
+    def spread_windows(a):
+        rt_copy(a, 1, 1, over).wait_recv()
+        for k in range(1, nv // 2):
+            rt_copy(a, 2 * k + 1, 1, view_at(2 * k)).start()
+
+    def send_windows(a):
+        for lane in range(lanes):
+            relay_copy(a, lane, source_at(lane, sibling)).wait_recv()
+            relay_copy(a, lane, source_at(lane, t)).wait_send()
+        for lane in range(1, lanes):
+            resid_copy(a, lane, t, t).wait_send()
         for k in range(2):
-            window = jnp.concatenate([resid_full[foot[a], a, k], resid_full[foot[a] + 1, a, k]], axis=0)
+            window = jnp.concatenate(
+                [resid_full[a][foot[a], k], resid_full[a][foot[a] + 1, k]], axis=0
+            )
             rt[0, k * rows : (k + 1) * rows, a * 2 * cols : (a + 1) * 2 * cols] = (
                 window.astype(jnp.float32).T.astype(jnp.bfloat16)
             )
-    rt_copies = []
-    for k in range(1, nv):
-        copy = remote(rt.at[0], rt.at[k], rt_send.at[k - 1], rt_recv.at[k - 1], view_at(k), t)
-        copy.start()
-        rt_copies.append(copy)
+        rt_copy(a, 1, 0, over).start()
+        for k in range(1, nv // 2):
+            rt_copy(a, 2 * k, 0, view_at(2 * k)).start()
+
+    batches = slots // BATCH
+    loads[2].wait()
+    run_patches(0, 0, batches)
+    send_update(0)
+    pump_some(PUMP[3])
+    share_sums()
+    loads[3].wait()
+    run_patches(1, 0, batches // 2)
+    for step in range(1, group):
+        group_copy(step).wait()
+    finish_object(0)
+    send_resid(0)
+    pump_some(PUMP[4])
+    run_patches(1, batches // 2, batches)
+    send_update(1)
+    pump_some(PUMP[5])
+    relay_resid(0)
+    send_windows(0)
+    pump_some(PUMP[6])
+    spread_windows(0)
+    finish_object(1)
+    send_resid(1)
+    pump_some(PUMP[7])
+    relay_resid(1)
+    send_windows(1)
+    pump_some(pieces)
+    spread_windows(1)
 
     own = weights_v[:, :, pl.ds(pl.multiple_of(v * span, span), span)]
     grad[...] = dot(rt[0], own.reshape(views * 2 * cols, span))
-    for k in range(1, nv):
-        weight_copies[k - 1].wait()
-        rt_copies[k - 1].wait()
-        grad[...] += dot(rt[k], weights_in[k - 1].reshape(views * 2 * cols, span))
+    for lane in range(1, nv):
+        for a in range(views):
+            if lane > 1:
+                rt_copy(a, lane, 0, v).wait_recv()
+            rt_copy(a, lane, 0, v).wait_send()
+        k = lane
+        remote(
+            weights_hbm.at[:, :, pl.ds(0, span)],
+            weights_in.at[k - 1],
+            w_send.at[k - 1],
+            w_recv.at[k - 1],
+            view_at(k),
+            t,
+        ).wait()
+        grad[...] += dot(rt[lane], weights_in[k - 1].reshape(views * 2 * cols, span))
 
     for c in range(share_cols):
         for k in range(2):
@@ -492,27 +633,86 @@
             halo_in[1, k].astype(jnp.float32) * has_fore,
         )
 
-    ag_copies = []
-    for k in range(1, nv):
-        copy = remote(
-            share, gathered.at[v], ag_send.at[k - 1], ag_recv.at[k - 1], view_at(k), t
-        )
+    up, down, across = view_at(2), view_at(-2), view_at(4)
+
+    def hand_on(source, k, lane, to):
+        return remote(
+            gathered.at[source, k],
+            gathered.at[source, k],
+            ag_send.at[lane, k],
+            ag_recv.at[lane, k],
+            to,
+            t,
+        )
+
+    other_up, other_down = lax.rem(over + 2, nv), lax.rem(over - 2 + nv, nv)
+    other_across = lax.rem(over + 4, nv)
+    sent = []
+
+    def go(copy):
         copy.start()
-        ag_copies.append(copy)
-    own_copy = pltpu.make_async_copy(share, gathered.at[v], ag_local)
+        sent.append(copy)
+
+    def own(k, lane, to):
+        return remote(
+            share.at[k], gathered.at[v, k], ag_send.at[lane, k], ag_recv.at[lane, k], to, t
+        )
+
+    own_copy = pltpu.make_async_copy(share, gathered.at[v], local_sem.at[5 + views])
+    for k in range(2):
+        go(own(k, 0, up))
+        go(own(k, 1, down))
+        go(own(k, 2, over))
     own_copy.start()
-    for k in range(1, nv):
-        source = view_at(-k)
-        remote(
-            share, gathered.at[source], ag_send.at[k - 1], ag_recv.at[k - 1], source, t
-        ).wait_recv()
-    for copy in ag_copies:
+    for k in range(2):
+        if k == 0:
+            hand_on(down, 0, 0, up).wait_recv()
+            go(hand_on(down, 0, 3, up))
+        else:
+            hand_on(up, 1, 1, down).wait_recv()
+            go(hand_on(up, 1, 3, down))
+        hand_on(over, k, 2, over).wait_recv()
+        go(hand_on(over, k, 4, up))
+        go(hand_on(over, k, 5, down))
+    for k in range(2):
+        hand_on(across, k, 3, up).wait_recv()
+        go(hand_on(across, k, 6, over))
+    hand_on(down, 1, 0, up).wait_recv()
+    hand_on(up, 0, 1, up).wait_recv()
+    for k in range(2):
+        hand_on(other_down, k, 4, up).wait_recv()
+        hand_on(other_up, k, 5, down).wait_recv()
+        hand_on(other_across, k, 6, over).wait_recv()
+    for copy in sent:
         copy.wait_send()
     own_copy.wait()
 
 
-def widen_kernel(x_ref, o_ref):
-    o_ref[...] = x_ref[0].astype(jnp.float32)
+def widen_kernel(object_ref, dual_ref, gathered, object_out, dual_out, volume_out, low, wide, in_sem, out_sem):
+    parts, _, share_cols = gathered.shape[:3]
+
+    def load(i):
+        return pltpu.make_async_copy(gathered.at[i], low.at[i], in_sem.at[i])
+
+    def store(i):
+        return pltpu.make_async_copy(
+            wide.at[i], volume_out.at[:, pl.ds(i * share_cols, share_cols)], out_sem.at[i]
+        )
+
+    for i in range(parts):
+        load(i).start()
+    object_out[...] = object_ref[...]
+    dual_out[...] = dual_ref[...]
+
+    def step(i, _):
+        load(i).wait()
+        wide[i] = low[i].astype(jnp.float32)
+        store(i).start()
+        return 0
+
+    lax.fori_loop(0, parts, step, 0)
+    for i in range(parts):
+        store(i).wait()
 
 
 def per_device(
@@ -535,12 +735,12 @@
     share_cols = cols // nv
     span = share_cols * depth
     minus, plus = dft_tables(pw)
-    any_space = pl.BlockSpec(memory_space=pl.ANY)
+    hbm = pl.BlockSpec(memory_space=pltpu.HBM)
     smem = pl.BlockSpec(memory_space=pltpu.SMEM)
     vmem = pl.BlockSpec(memory_space=pltpu.VMEM)
     bf16, f32 = jnp.bfloat16, jnp.float32
     dma = pltpu.SemaphoreType.DMA
-    chips = nt // 2
+    levels = nt // 4
     band = jax.ShapeDtypeStruct(object_band.shape, f32)
     object_new, dual_new, gathered = pl.pallas_call(
         functools.partial(front_kernel, nv, nt),
@@ -549,9 +749,12 @@
             band,
             jax.ShapeDtypeStruct((nv, 2, share_cols, depth, rows), bf16),
         ),
-        in_specs=[smem] * 3 + [any_space] * 2 + [vmem] * 3 + [any_space] * 3,
-        out_specs=(vmem, vmem, any_space),
+        in_specs=[smem] * 3 + [hbm] * 8,
+        out_specs=(vmem, vmem, hbm),
         scratch_shapes=[
+            pltpu.VMEM(probe_field.shape, f32),
+            pltpu.VMEM(minus.shape, bf16),
+            pltpu.VMEM(plus.shape, bf16),
             pltpu.VMEM((views, 2, cols, rows), f32),
             pltpu.VMEM((views, 2, 3 * cols, rows), f32),
             pltpu.VMEM((views, slots, pw, rows), jnp.int32),
@@ -559,50 +762,54 @@
             pltpu.VMEM(volume.shape, f32),
             pltpu.VMEM((nv - 1, views, 2 * cols, span), bf16),
             pltpu.VMEM((views * 2 * cols, 2 * rows), f32),
-            pltpu.VMEM((nt - 1, views, 2, cols, rows), bf16),
-            pltpu.VMEM((nt - 1, views, 2, cols, rows), bf16),
+            pltpu.VMEM((levels - 1, 4, views, 2, cols, rows), bf16),
+            pltpu.VMEM((levels - 1, 4, views, 2, cols, rows), bf16),
+            pltpu.VMEM((3, views, 2, cols, rows), bf16),
+            pltpu.VMEM((3, views, 2, cols, rows), bf16),
             pltpu.VMEM((BATCH, 2, 4 * cols, rows), f32),
             pltpu.VMEM((4 * cols, rows), f32),
             pltpu.VMEM((views, 3, 3 * cols, rows), f32),
             pltpu.VMEM((views, 2, 3, cols, rows), bf16),
             pltpu.VMEM((views, 2, 3, cols, rows), bf16),
-            pltpu.VMEM((nt, views, 2, cols, rows), bf16),
+            pltpu.VMEM((nt, 2, cols, rows), bf16),
+            pltpu.VMEM((nt, 2, cols, rows), bf16),
             pltpu.VMEM((nv, 2 * rows, views * 2 * cols), bf16),
             pltpu.VMEM((2 * rows, span), f32),
             pltpu.VMEM((2, share_cols, depth, rows), f32),
             pltpu.VMEM((2, 2, depth, rows), bf16),
             pltpu.VMEM((2, 2, depth, rows), bf16),
             pltpu.VMEM((2, share_cols, depth, rows), bf16),
-            dma((2 + views,)),
+            dma((6 + views,)),
             dma((2, nv)),
             dma((nv - 1,)),
             dma((nv - 1,)),
             dma((2,)),
             dma((2,)),
-            dma((nt - 1,)),
-            dma((nt - 1,)),
+            dma((levels - 1,)),
+            dma((levels - 1,)),
+            dma((3,)),
+            dma((3,)),
             dma((views, 2)),
             dma((views, 2)),
-            dma((chips,)),
-            dma((chips,)),
-            dma((chips - 1,)),
-            dma((chips - 1,)),
-            dma((nv - 1,)),
-            dma((nv - 1,)),
+            dma((views, 2 * levels)),
+            dma((views, 2 * levels)),
+            dma((views, 2 * levels)),
+            dma((views, 2 * levels)),
+            dma((views, nv - 1)),
+            dma((views, nv - 1)),
             dma((2,)),
             dma((2,)),
-            dma((nv - 1,)),
-            dma((nv - 1,)),
-            dma(()),
+            dma((7, 2)),
+            dma((7, 2)),
         ],
         compiler_params=pltpu.CompilerParams(
-            collective_id=0, has_side_effects=True, vmem_limit_bytes=52 * MIB
+            collective_id=0, has_side_effects=True, vmem_limit_bytes=FRONT_VMEM * MIB
         ),
         name="front",
     )(
         positions,
-        live_counts,
-        footprints,
+        live_counts.reshape(views),
+        footprints.reshape(views),
         object_band,
         dual_band,
         probe_field,
@@ -612,16 +819,20 @@
         weights,
         volume,
     )
-    volume_new = pl.pallas_call(
+    return pl.pallas_call(
         widen_kernel,
-        grid=(nv,),
-        out_shape=jax.ShapeDtypeStruct(volume.shape, f32),
-        in_specs=[pl.BlockSpec((1, 2, share_cols, depth, rows), lambda i: (i, 0, 0, 0, 0))],
-        out_specs=pl.BlockSpec((2, share_cols, depth, rows), lambda i: (0, i, 0, 0)),
-        compiler_params=pltpu.CompilerParams(vmem_limit_bytes=32 * MIB),
+        out_shape=(band, band, jax.ShapeDtypeStruct(volume.shape, f32)),
+        in_specs=[vmem, vmem, hbm],
+        out_specs=(vmem, vmem, hbm),
+        scratch_shapes=[
+            pltpu.VMEM(gathered.shape, bf16),
+            pltpu.VMEM(gathered.shape, f32),
+            dma((nv,)),
+            dma((nv,)),
+        ],
+        compiler_params=pltpu.CompilerParams(vmem_limit_bytes=WIDEN_VMEM * MIB),
         name="widen",
-    )(gathered)
-    return object_new, dual_new, volume_new
+    )(object_new, dual_new, gathered)
 
 
 def solution(mesh):

time: 173 us -> 135 us (0.78)
  Pallas kernels: 162 us -> 133 us
  local copies, waits for them, and re-layouts: 10.2 us -> 0 us
    pallas_call x1, Pallas kernels: 157 us -> 127 us  [per_device(): pl.pallas_call(functools.partial(front_kernel, nv, nt), out_shape=(band,...]
    unnamed x18 -> x0, local copies, waits for them, and re-layouts: 10.2 us -> none
where the time goes in v2:
time: 135 us; the launch traced here: 134 us
  Pallas kernels  133 us (99%)
    pallas_call x1, Pallas kernels, per_device(): pl.pallas_call(functools.partial(front_kernel, nv, nt), out_shape=(band,...  127 us
    pallas_call x1, Pallas kernels, per_device(): pl.pallas_call(widen_kernel, out_shape=(band, band, jax.ShapeDtypeStruct(...  6.21 us

profile of v2, /device:TPU:1, one launch (start us, length us, event | category | flops | bytes accessed | tf_op | source)
XLA Modules:
  0.0 134.1 jit_solution(13258026238003933334)
XLA Ops:
  0.6 127.2 %front.1 = (f32[2,2,64,128]{3,2,1,0:T(8,128)}, f32[2,2,64,128]{3,2,1,0:T(8,128)}, bf16[8,2,8,128,128]{4,3,2,1,0:T(8,128)(2,1)}) custom-call(s32[2,32]{1,0:T(2,128)} %positions.1, s32[2]{0:T(128)} %bitcast.2, s32[2]{0:T(128)} %bitcast.3, f32[2,2,64,128]{3,2,1,0:T(8,128)} %object_hbm.1, f32[2,2,64,128]{3,2,1,0:T(8,128)} %dual_hbm.1, f32[2,128,128]{2,1,0:T(8,128)} %probe_hbm.1, ...), custom_call_target="tpu_custom_call" | custom-call | tf_op jit(solution)/shard_map/front/pallas_call | solution.py:745
  127.8 6.2 %widen.1 = (f32[2,2,64,128]{3,2,1,0:T(8,128)}, f32[2,2,64,128]{3,2,1,0:T(8,128)}, f32[2,64,128,128]{3,2,1,0:T(8,128)}) custom-call(f32[2,2,64,128]{3,2,1,0:T(8,128)} %get-tuple-element.6.object_ref, f32[2,2,64,128]{3,2,1,0:T(8,128)} %get-tuple-element.7.dual_ref, bf16[8,2,8,128,128]{4,3,2,1,0:T(8,128)(2,1)} %get-tuple-element.8.gathered), custom_call_target="tpu_custom_call" | custom-call | tf_op jit(solution)/shard_map/widen/pallas_call | solution.py:822

commit v3 on v2

--- a/solution.py
+++ b/solution.py
@@ -15,7 +15,7 @@
 BATCH = 4
 FRONT_VMEM = 60
 WIDEN_VMEM = 60
-PUMP = (11, 4, 2, 4, 4, 4, 4, 4)
+PUMP = (10, 4, 1, 4, 6, 6, 4)
 MIB = 2**20
 
 
@@ -275,51 +275,50 @@
             foot[a] + 1 == to
         )
 
-    def level_copy(k):
+    def level_copy(k, a):
         return remote(
-            shadow_out.at[k - 1],
-            shadow_in.at[k - 1],
-            sh_send.at[k - 1],
-            sh_recv.at[k - 1],
+            shadow_out.at[k - 1, a],
+            shadow_in.at[k - 1, a],
+            sh_send.at[k - 1, a],
+            sh_recv.at[k - 1, a],
             v,
             level_at(k) * group + place,
         )
 
-    def group_copy(k):
+    def group_copy(k, a):
         return remote(
-            shared_out.at[k - 1],
-            shared_in.at[k - 1],
-            gr_send.at[k - 1],
-            gr_recv.at[k - 1],
+            shared_out.at[k - 1, a],
+            shared_in.at[k - 1, a],
+            gr_send.at[k - 1, a],
+            gr_recv.at[k - 1, a],
             v,
             z * group + lax.rem(place + k, group),
         )
 
-    for step in range(1, levels):
-        for k in range(group):
-            to = level_at(step) * group + k
-            for a in range(views):
+    for a in range(views):
+        for step in range(1, levels):
+            for k in range(group):
+                to = level_at(step) * group + k
                 for plane in range(2):
-                    shadow_out[step - 1, k, a, plane] = placed(to, a, plane).astype(jnp.bfloat16)
-        level_copy(step).start()
+                    shadow_out[step - 1, a, k, plane] = placed(to, a, plane).astype(jnp.bfloat16)
+            level_copy(step, a).start()
 
     def level_sum(to, k, a, plane):
         total = placed(to, a, plane)
         for step in range(1, levels):
-            total = total + shadow_in[step - 1, k, a, plane].astype(jnp.float32)
+            total = total + shadow_in[step - 1, a, k, plane].astype(jnp.float32)
         return total
 
-    def share_sums():
+    def share_sums(a):
         for step in range(1, levels):
-            level_copy(step).wait()
+            level_copy(step, a).wait()
         for step in range(1, group):
             k = lax.rem(place + step, group)
-            for a in range(views):
-                for plane in range(2):
-                    shared_out[step - 1, a, plane] = level_sum(
-                        z * group + k, k, a, plane
-                    ).astype(jnp.bfloat16)
-            group_copy(step).start()
+            for plane in range(2):
+                shared_out[step - 1, a, plane] = level_sum(z * group + k, k, a, plane).astype(
+                    jnp.bfloat16
+                )
+            group_copy(step, a).start()
 
     pump_some(PUMP[1])
 
@@ -438,6 +437,8 @@
     from_one, from_two = flag(t >= 1), flag(t >= 2)
 
     def finish_object(a):
+        for step in range(1, group):
+            group_copy(step, a).wait()
         for k in (1, 2):
             update_copy(a, k).wait()
         upd = (
@@ -538,36 +539,29 @@
             rt_copy(a, 2 * k, 0, view_at(2 * k)).start()
 
     batches = slots // BATCH
-    loads[2].wait()
-    run_patches(0, 0, batches)
-    send_update(0)
+    for a in range(views):
+        loads[2 + a].wait()
+        run_patches(a, 0, batches)
+        send_update(a)
+        share_sums(a)
     pump_some(PUMP[3])
-    share_sums()
-    loads[3].wait()
-    run_patches(1, 0, batches // 2)
-    for step in range(1, group):
-        group_copy(step).wait()
-    finish_object(0)
-    send_resid(0)
+    for a in range(views):
+        finish_object(a)
+        send_resid(a)
     pump_some(PUMP[4])
-    run_patches(1, batches // 2, batches)
-    send_update(1)
+    for a in range(views):
+        relay_resid(a)
     pump_some(PUMP[5])
-    relay_resid(0)
-    send_windows(0)
+    for a in range(views):
+        send_windows(a)
     pump_some(PUMP[6])
-    spread_windows(0)
-    finish_object(1)
-    send_resid(1)
-    pump_some(PUMP[7])
-    relay_resid(1)
-    send_windows(1)
+    for a in range(views):
+        spread_windows(a)
     pump_some(pieces)
-    spread_windows(1)
 
     own = weights_v[:, :, pl.ds(pl.multiple_of(v * span, span), span)]
     grad[...] = dot(rt[0], own.reshape(views * 2 * cols, span))
-    for lane in range(1, nv):
+    for lane in (1, *range(2, nv, 2), *range(3, nv, 2)):
         for a in range(views):
             if lane > 1:
                 rt_copy(a, lane, 0, v).wait_recv()
@@ -608,81 +602,94 @@
         right = jnp.where(lane == rows - 1, 0.0, pltpu.roll(x, rows - 1, 1))
         return phi(x - below) + phi(x - above) + phi(x - left) + phi(x - right)
 
-    def finish(k, c, before, after):
+    def finish(k, c, slot, before, after):
         x = half[k, c]
         prior = inner(x) + phi(x - before) + phi(x - after)
-        share[k, c] = (x - (step_size * prior_weight) * prior).astype(jnp.bfloat16)
+        share[k, slot] = (x - (step_size * prior_weight) * prior).astype(jnp.bfloat16)
+
+    up, down, across = view_at(2), view_at(-2), view_at(4)
+    other_up, other_down = lax.rem(over + 2, nv), lax.rem(over - 2 + nv, nv)
+    other_across = lax.rem(over + 4, nv)
+    inner_cols = share_cols - 2
+    spans = (pl.ds(0, inner_cols), pl.ds(inner_cols, 2))
+    sent = []
+
+    def go(copy):
+        copy.start()
+        sent.append(copy)
+
+    def hand_on(source, k, part, lane, to):
+        return remote(
+            gathered.at[source, k, spans[part]],
+            gathered.at[source, k, spans[part]],
+            ag_send.at[lane, k, part],
+            ag_recv.at[lane, k, part],
+            to,
+            t,
+        )
+
+    def own(k, part, lane, to):
+        return remote(
+            share.at[k, spans[part]],
+            gathered.at[v, k, spans[part]],
+            ag_send.at[lane, k, part],
+            ag_recv.at[lane, k, part],
+            to,
+            t,
+        )
+
+    def send_own(k, part):
+        go(own(k, part, 0, up))
+        go(own(k, part, 1, down))
+        go(own(k, part, 2, over))
 
     for k in range(2):
         lax.fori_loop(
             1,
             share_cols - 1,
-            lambda c, _, k=k: (finish(k, c, half[k, c - 1], half[k, c + 1]), 0)[1],
+            lambda c, _, k=k: (finish(k, c, c - 1, half[k, c - 1], half[k, c + 1]), 0)[1],
             0,
         )
+        send_own(k, 0)
     for copy in halo_copies:
         copy.wait()
     has_back = flag((v > 0) | (t > 0))
     has_fore = flag((v < nv - 1) | (t < nt - 1))
     for k in range(2):
-        finish(k, 0, halo_in[0, k].astype(jnp.float32) * has_back, half[k, 1])
+        finish(k, 0, share_cols - 2, halo_in[0, k].astype(jnp.float32) * has_back, half[k, 1])
         finish(
             k,
             share_cols - 1,
+            share_cols - 1,
             half[k, share_cols - 2],
             halo_in[1, k].astype(jnp.float32) * has_fore,
         )
-
-    up, down, across = view_at(2), view_at(-2), view_at(4)
-
-    def hand_on(source, k, lane, to):
-        return remote(
-            gathered.at[source, k],
-            gathered.at[source, k],
-            ag_send.at[lane, k],
-            ag_recv.at[lane, k],
-            to,
-            t,
-        )
-
-    other_up, other_down = lax.rem(over + 2, nv), lax.rem(over - 2 + nv, nv)
-    other_across = lax.rem(over + 4, nv)
-    sent = []
-
-    def go(copy):
-        copy.start()
-        sent.append(copy)
-
-    def own(k, lane, to):
-        return remote(
-            share.at[k], gathered.at[v, k], ag_send.at[lane, k], ag_recv.at[lane, k], to, t
-        )
+        send_own(k, 1)
 
     own_copy = pltpu.make_async_copy(share, gathered.at[v], local_sem.at[5 + views])
-    for k in range(2):
-        go(own(k, 0, up))
-        go(own(k, 1, down))
-        go(own(k, 2, over))
     own_copy.start()
-    for k in range(2):
-        if k == 0:
-            hand_on(down, 0, 0, up).wait_recv()
-            go(hand_on(down, 0, 3, up))
-        else:
-            hand_on(up, 1, 1, down).wait_recv()
-            go(hand_on(up, 1, 3, down))
-        hand_on(over, k, 2, over).wait_recv()
-        go(hand_on(over, k, 4, up))
-        go(hand_on(over, k, 5, down))
-    for k in range(2):
-        hand_on(across, k, 3, up).wait_recv()
-        go(hand_on(across, k, 6, over))
-    hand_on(down, 1, 0, up).wait_recv()
-    hand_on(up, 0, 1, up).wait_recv()
-    for k in range(2):
-        hand_on(other_down, k, 4, up).wait_recv()
-        hand_on(other_up, k, 5, down).wait_recv()
-        hand_on(other_across, k, 6, over).wait_recv()
+    for part in range(2):
+        for k in range(2):
+            if k == 0:
+                hand_on(down, 0, part, 0, up).wait_recv()
+                go(hand_on(down, 0, part, 3, up))
+            else:
+                hand_on(up, 1, part, 1, down).wait_recv()
+                go(hand_on(up, 1, part, 3, down))
+            hand_on(over, k, part, 2, over).wait_recv()
+            go(hand_on(over, k, part, 4, up))
+            go(hand_on(over, k, part, 5, down))
+    for part in range(2):
+        for k in range(2):
+            hand_on(across, k, part, 3, up).wait_recv()
+            go(hand_on(across, k, part, 6, over))
+    for part in range(2):
+        hand_on(down, 1, part, 0, up).wait_recv()
+        hand_on(up, 0, part, 1, up).wait_recv()
+        for k in range(2):
+            hand_on(other_down, k, part, 4, up).wait_recv()
+            hand_on(other_up, k, part, 5, down).wait_recv()
+            hand_on(other_across, k, part, 6, over).wait_recv()
     for copy in sent:
         copy.wait_send()
     own_copy.wait()
@@ -706,7 +713,9 @@
 
     def step(i, _):
         load(i).wait()
-        wide[i] = low[i].astype(jnp.float32)
+        wide[i, :, 1 : share_cols - 1] = low[i, :, : share_cols - 2].astype(jnp.float32)
+        wide[i, :, 0] = low[i, :, share_cols - 2].astype(jnp.float32)
+        wide[i, :, share_cols - 1] = low[i, :, share_cols - 1].astype(jnp.float32)
         store(i).start()
         return 0
 
@@ -762,8 +771,8 @@
             pltpu.VMEM(volume.shape, f32),
             pltpu.VMEM((nv - 1, views, 2 * cols, span), bf16),
             pltpu.VMEM((views * 2 * cols, 2 * rows), f32),
-            pltpu.VMEM((levels - 1, 4, views, 2, cols, rows), bf16),
-            pltpu.VMEM((levels - 1, 4, views, 2, cols, rows), bf16),
+            pltpu.VMEM((levels - 1, views, 4, 2, cols, rows), bf16),
+            pltpu.VMEM((levels - 1, views, 4, 2, cols, rows), bf16),
             pltpu.VMEM((3, views, 2, cols, rows), bf16),
             pltpu.VMEM((3, views, 2, cols, rows), bf16),
             pltpu.VMEM((BATCH, 2, 4 * cols, rows), f32),
@@ -785,10 +794,10 @@
             dma((nv - 1,)),
             dma((2,)),
             dma((2,)),
-            dma((levels - 1,)),
-            dma((levels - 1,)),
-            dma((3,)),
-            dma((3,)),
+            dma((levels - 1, views)),
+            dma((levels - 1, views)),
+            dma((3, views)),
+            dma((3, views)),
             dma((views, 2)),
             dma((views, 2)),
             dma((views, 2 * levels)),
@@ -799,8 +808,8 @@
             dma((views, nv - 1)),
             dma((2,)),
             dma((2,)),
-            dma((7, 2)),
-            dma((7, 2)),
+            dma((7, 2, 2)),
+            dma((7, 2, 2)),
         ],
         compiler_params=pltpu.CompilerParams(
             collective_id=0, has_side_effects=True, vmem_limit_bytes=FRONT_VMEM * MIB

time: 135 us -> 128 us (0.948)
  Pallas kernels: 133 us -> 128 us
    pallas_call x1, Pallas kernels: 127 us -> 121 us  [per_device(): pl.pallas_call(functools.partial(front_kernel, nv, nt), out_shape=(band,...]
where the time goes in v3:
time: 128 us
  Pallas kernels  128 us (100%)
    pallas_call x1, Pallas kernels, per_device(): pl.pallas_call(functools.partial(front_kernel, nv, nt), out_shape=(band,...  121 us
    pallas_call x1, Pallas kernels, per_device(): pl.pallas_call(widen_kernel, out_shape=(band, band, jax.ShapeDtypeStruct(...  6.21 us

profile of v3, /device:TPU:1, one launch (start us, length us, event | category | flops | bytes accessed | tf_op | source)
XLA Modules:
  0.0 128.3 jit_solution(7812292464184726792)
XLA Ops:
  0.6 121.4 %front.1 = (f32[2,2,64,128]{3,2,1,0:T(8,128)}, f32[2,2,64,128]{3,2,1,0:T(8,128)}, bf16[8,2,8,128,128]{4,3,2,1,0:T(8,128)(2,1)}) custom-call(s32[2,32]{1,0:T(2,128)} %positions.1, s32[2]{0:T(128)} %bitcast.2, s32[2]{0:T(128)} %bitcast.3, f32[2,2,64,128]{3,2,1,0:T(8,128)} %object_hbm.1, f32[2,2,64,128]{3,2,1,0:T(8,128)} %dual_hbm.1, f32[2,128,128]{2,1,0:T(8,128)} %probe_hbm.1, ...), custom_call_target="tpu_custom_call" | custom-call | tf_op jit(solution)/shard_map/front/pallas_call | solution.py:754
  122.1 6.2 %widen.1 = (f32[2,2,64,128]{3,2,1,0:T(8,128)}, f32[2,2,64,128]{3,2,1,0:T(8,128)}, f32[2,64,128,128]{3,2,1,0:T(8,128)}) custom-call(f32[2,2,64,128]{3,2,1,0:T(8,128)} %get-tuple-element.6.object_ref, f32[2,2,64,128]{3,2,1,0:T(8,128)} %get-tuple-element.7.dual_ref, bf16[8,2,8,128,128]{4,3,2,1,0:T(8,128)(2,1)} %get-tuple-element.8.gathered), custom_call_target="tpu_custom_call" | custom-call | tf_op jit(solution)/shard_map/widen/pallas_call | solution.py:831

commit v4 on v3

--- a/solution.py
+++ b/solution.py
@@ -13,9 +13,10 @@
 prior_weight = 0.5
 MESH = pl.DeviceIdType.MESH
 BATCH = 4
+PIECE_ROWS = 16
 FRONT_VMEM = 60
 WIDEN_VMEM = 60
-PUMP = (10, 4, 1, 4, 6, 6, 4)
+PUMP = (16, 6, 1, 2, 4, 4)
 MIB = 2**20
 
 
@@ -82,6 +83,8 @@
     resid_second,
     rt,
     grad,
+    pair_out,
+    pair_in,
     half,
     halo_out,
     halo_in,
@@ -104,6 +107,8 @@
     rel_recv,
     rt_send,
     rt_recv,
+    pair_send,
+    pair_recv,
     halo_send,
     halo_recv,
     ag_send,
@@ -215,8 +220,9 @@
     for copy in object_copies:
         copy.start()
 
-    peers = nv - 1
-    piece_rows = 32
+    peers = nv // 2 - 1
+    piece_rows = PIECE_ROWS
+    wide_span = 2 * span
     per_view = 2 * cols // piece_rows
     pieces = peers * views * per_view
 
@@ -227,10 +233,10 @@
             row_block = index // peers
             a = row_block // per_view
             rows_at = pl.multiple_of((row_block % per_view) * piece_rows, piece_rows)
-            lane = k + 1
-            to = lax.rem(v - view_x + 2 * (lane // 2), nv) + lax.rem(view_x + lane, 2)
+            to = lax.rem(v + 2 * (k + 1), nv)
+            first_voxel = pl.multiple_of((to // 2) * wide_span, wide_span)
             remote(
-                weights_hbm.at[a, pl.ds(rows_at, piece_rows), pl.ds(pl.multiple_of(to * span, span), span)],
+                weights_hbm.at[a, pl.ds(rows_at, piece_rows), pl.ds(first_voxel, wide_span)],
                 weights_in.at[k, a, pl.ds(rows_at, piece_rows), :],
                 w_send.at[k],
                 w_recv.at[k],
@@ -506,20 +512,15 @@
     def rt_part(k, a):
         return rt.at[k, :, pl.ds(a * 2 * cols, 2 * cols)]
 
-    def rt_copy(a, lane, k, to):
+    def rt_copy(a, lane, to):
         return remote(
-            rt_part(k, a),
+            rt_part(0, a),
             rt_part(lane, a),
             rt_send.at[a, lane - 1],
             rt_recv.at[a, lane - 1],
             to,
             t,
         )
-
-    def spread_windows(a):
-        rt_copy(a, 1, 1, over).wait_recv()
-        for k in range(1, nv // 2):
-            rt_copy(a, 2 * k + 1, 1, view_at(2 * k)).start()
 
     def send_windows(a):
         for lane in range(lanes):
@@ -534,9 +535,8 @@
             rt[0, k * rows : (k + 1) * rows, a * 2 * cols : (a + 1) * 2 * cols] = (
                 window.astype(jnp.float32).T.astype(jnp.bfloat16)
             )
-        rt_copy(a, 1, 0, over).start()
         for k in range(1, nv // 2):
-            rt_copy(a, 2 * k, 0, view_at(2 * k)).start()
+            rt_copy(a, k, view_at(2 * k)).start()
 
     batches = slots // BATCH
     for a in range(views):
@@ -554,34 +554,123 @@
     pump_some(PUMP[5])
     for a in range(views):
         send_windows(a)
-    pump_some(PUMP[6])
-    for a in range(views):
-        spread_windows(a)
     pump_some(pieces)
 
-    own = weights_v[:, :, pl.ds(pl.multiple_of(v * span, span), span)]
-    grad[...] = dot(rt[0], own.reshape(views * 2 * cols, span))
-    for lane in (1, *range(2, nv, 2), *range(3, nv, 2)):
+    base = pl.multiple_of((v // 2) * wide_span, wide_span)
+
+    def product(lane, side):
+        at = pl.multiple_of(side * span, span)
+        if lane:
+            block = weights_in[lane - 1, :, :, pl.ds(at, span)]
+        else:
+            block = weights_v[:, :, pl.ds(base + at, span)]
+        return dot(rt[lane], block.reshape(views * 2 * cols, span))
+
+    grad[0] = product(0, 1 - view_x)
+    grad[1] = product(0, view_x)
+    for lane in range(1, nv // 2):
         for a in range(views):
-            if lane > 1:
-                rt_copy(a, lane, 0, v).wait_recv()
-            rt_copy(a, lane, 0, v).wait_send()
-        k = lane
+            rt_copy(a, lane, v).wait()
         remote(
-            weights_hbm.at[:, :, pl.ds(0, span)],
-            weights_in.at[k - 1],
-            w_send.at[k - 1],
-            w_recv.at[k - 1],
-            view_at(k),
+            weights_hbm.at[:, :, pl.ds(0, wide_span)],
+            weights_in.at[lane - 1],
+            w_send.at[lane - 1],
+            w_recv.at[lane - 1],
+            v,
             t,
         ).wait()
-        grad[...] += dot(rt[lane], weights_in[k - 1].reshape(views * 2 * cols, span))
-
-    for c in range(share_cols):
-        for k in range(2):
-            part = grad[k * rows : (k + 1) * rows, c * depth : (c + 1) * depth].T
-            half[k, c] = volume_v[k, v * share_cols + c] - step_size * part
-
+        grad[0] += product(lane, 1 - view_x)
+        if lane < nv // 2 - 1:
+            grad[1] += product(lane, view_x)
+
+    def pair_copy(part):
+        return remote(
+            pair_out.at[part], pair_in.at[part], pair_send.at[part], pair_recv.at[part], over, t
+        )
+
+    half_span = span // 2
+    for part in range(2):
+        pair_out[part] = grad[0, :, part * half_span : (part + 1) * half_span].astype(jnp.bfloat16)
+        pair_copy(part).start()
+    grad[1] += product(nv // 2 - 1, view_x)
+    def take_pair(part):
+        pair_copy(part).wait()
+        for c in range(part * share_cols // 2, (part + 1) * share_cols // 2):
+            in_part = c * depth - part * half_span
+            for k in range(2):
+                both = grad[1, k * rows : (k + 1) * rows, c * depth : (c + 1) * depth] + pair_in[
+                    part, k * rows : (k + 1) * rows, in_part : in_part + depth
+                ].astype(jnp.float32)
+                half[k, c] = volume_v[k, v * share_cols + c] - step_size * both.T
+
+    row = lax.broadcasted_iota(jnp.int32, (depth, rows), 0)
+    lane = lax.broadcasted_iota(jnp.int32, (depth, rows), 1)
+
+    def inner(x):
+        below = jnp.where(row == 0, 0.0, pltpu.roll(x, 1, 0))
+        above = jnp.where(row == depth - 1, 0.0, pltpu.roll(x, depth - 1, 0))
+        left = jnp.where(lane == 0, 0.0, pltpu.roll(x, 1, 1))
+        right = jnp.where(lane == rows - 1, 0.0, pltpu.roll(x, rows - 1, 1))
+        return phi(x - below) + phi(x - above) + phi(x - left) + phi(x - right)
+
+    def finish(k, c, slot, before, after):
+        x = half[k, c]
+        prior = inner(x) + phi(x - before) + phi(x - after)
+        share[k, slot] = (x - (step_size * prior_weight) * prior).astype(jnp.bfloat16)
+
+    up, down, across = view_at(2), view_at(-2), view_at(4)
+    other_up, other_down = lax.rem(over + 2, nv), lax.rem(over - 2 + nv, nv)
+    other_across = lax.rem(over + 4, nv)
+    early = share_cols // 2 - 2
+    spans = (
+        pl.ds(0, early),
+        pl.ds(early, share_cols - 2 - early),
+        pl.ds(share_cols - 2, 2),
+    )
+    sent = []
+
+    def go(copy):
+        copy.start()
+        sent.append(copy)
+
+    def hand_on(source, k, part, lane, to):
+        return remote(
+            gathered.at[source, k, spans[part]],
+            gathered.at[source, k, spans[part]],
+            ag_send.at[lane, k, part],
+            ag_recv.at[lane, k, part],
+            to,
+            t,
+        )
+
+    def own(k, part, lane, to):
+        return remote(
+            share.at[k, spans[part]],
+            gathered.at[v, k, spans[part]],
+            ag_send.at[lane, k, part],
+            ag_recv.at[lane, k, part],
+            to,
+            t,
+        )
+
+    def send_own(k, part):
+        go(own(k, part, 0, up))
+        go(own(k, part, 1, down))
+        go(own(k, part, 2, over))
+
+    def finish_inner(k, first, last):
+        lax.fori_loop(
+            first,
+            last,
+            lambda c, _: (finish(k, c, c - 1, half[k, c - 1], half[k, c + 1]), 0)[1],
+            0,
+        )
+
+    take_pair(0)
+    for k in range(2):
+        finish_inner(k, 1, early + 1)
+        send_own(k, 0)
+    take_pair(1)
     for k in range(2):
         halo_out[0, k] = half[k, 0].astype(jnp.bfloat16)
         halo_out[1, k] = half[k, share_cols - 1].astype(jnp.bfloat16)
@@ -591,66 +680,9 @@
     ]
     for copy in halo_copies:
         copy.start()
-
-    row = lax.broadcasted_iota(jnp.int32, (depth, rows), 0)
-    lane = lax.broadcasted_iota(jnp.int32, (depth, rows), 1)
-
-    def inner(x):
-        below = jnp.where(row == 0, 0.0, pltpu.roll(x, 1, 0))
-        above = jnp.where(row == depth - 1, 0.0, pltpu.roll(x, depth - 1, 0))
-        left = jnp.where(lane == 0, 0.0, pltpu.roll(x, 1, 1))
-        right = jnp.where(lane == rows - 1, 0.0, pltpu.roll(x, rows - 1, 1))
-        return phi(x - below) + phi(x - above) + phi(x - left) + phi(x - right)
-
-    def finish(k, c, slot, before, after):
-        x = half[k, c]
-        prior = inner(x) + phi(x - before) + phi(x - after)
-        share[k, slot] = (x - (step_size * prior_weight) * prior).astype(jnp.bfloat16)
-
-    up, down, across = view_at(2), view_at(-2), view_at(4)
-    other_up, other_down = lax.rem(over + 2, nv), lax.rem(over - 2 + nv, nv)
-    other_across = lax.rem(over + 4, nv)
-    inner_cols = share_cols - 2
-    spans = (pl.ds(0, inner_cols), pl.ds(inner_cols, 2))
-    sent = []
-
-    def go(copy):
-        copy.start()
-        sent.append(copy)
-
-    def hand_on(source, k, part, lane, to):
-        return remote(
-            gathered.at[source, k, spans[part]],
-            gathered.at[source, k, spans[part]],
-            ag_send.at[lane, k, part],
-            ag_recv.at[lane, k, part],
-            to,
-            t,
-        )
-
-    def own(k, part, lane, to):
-        return remote(
-            share.at[k, spans[part]],
-            gathered.at[v, k, spans[part]],
-            ag_send.at[lane, k, part],
-            ag_recv.at[lane, k, part],
-            to,
-            t,
-        )
-
-    def send_own(k, part):
-        go(own(k, part, 0, up))
-        go(own(k, part, 1, down))
-        go(own(k, part, 2, over))
-
     for k in range(2):
-        lax.fori_loop(
-            1,
-            share_cols - 1,
-            lambda c, _, k=k: (finish(k, c, c - 1, half[k, c - 1], half[k, c + 1]), 0)[1],
-            0,
-        )
-        send_own(k, 0)
+        finish_inner(k, early + 1, share_cols - 1)
+        send_own(k, 1)
     for copy in halo_copies:
         copy.wait()
     has_back = flag((v > 0) | (t > 0))
@@ -664,11 +696,11 @@
             half[k, share_cols - 2],
             halo_in[1, k].astype(jnp.float32) * has_fore,
         )
-        send_own(k, 1)
+        send_own(k, 2)
 
     own_copy = pltpu.make_async_copy(share, gathered.at[v], local_sem.at[5 + views])
     own_copy.start()
-    for part in range(2):
+    for part in range(3):
         for k in range(2):
             if k == 0:
                 hand_on(down, 0, part, 0, up).wait_recv()
@@ -679,11 +711,11 @@
             hand_on(over, k, part, 2, over).wait_recv()
             go(hand_on(over, k, part, 4, up))
             go(hand_on(over, k, part, 5, down))
-    for part in range(2):
+    for part in range(3):
         for k in range(2):
             hand_on(across, k, part, 3, up).wait_recv()
             go(hand_on(across, k, part, 6, over))
-    for part in range(2):
+    for part in range(3):
         hand_on(down, 1, part, 0, up).wait_recv()
         hand_on(up, 0, part, 1, up).wait_recv()
         for k in range(2):
@@ -769,7 +801,7 @@
             pltpu.VMEM((views, slots, pw, rows), jnp.int32),
             pltpu.VMEM(weights.shape, bf16),
             pltpu.VMEM(volume.shape, f32),
-            pltpu.VMEM((nv - 1, views, 2 * cols, span), bf16),
+            pltpu.VMEM((nv // 2 - 1, views, 2 * cols, 2 * span), bf16),
             pltpu.VMEM((views * 2 * cols, 2 * rows), f32),
             pltpu.VMEM((levels - 1, views, 4, 2, cols, rows), bf16),
             pltpu.VMEM((levels - 1, views, 4, 2, cols, rows), bf16),
@@ -782,16 +814,18 @@
             pltpu.VMEM((views, 2, 3, cols, rows), bf16),
             pltpu.VMEM((nt, 2, cols, rows), bf16),
             pltpu.VMEM((nt, 2, cols, rows), bf16),
-            pltpu.VMEM((nv, 2 * rows, views * 2 * cols), bf16),
-            pltpu.VMEM((2 * rows, span), f32),
+            pltpu.VMEM((nv // 2, 2 * rows, views * 2 * cols), bf16),
+            pltpu.VMEM((2, 2 * rows, span), f32),
+            pltpu.VMEM((2, 2 * rows, span // 2), bf16),
+            pltpu.VMEM((2, 2 * rows, span // 2), bf16),
             pltpu.VMEM((2, share_cols, depth, rows), f32),
             pltpu.VMEM((2, 2, depth, rows), bf16),
             pltpu.VMEM((2, 2, depth, rows), bf16),
             pltpu.VMEM((2, share_cols, depth, rows), bf16),
             dma((6 + views,)),
             dma((2, nv)),
-            dma((nv - 1,)),
-            dma((nv - 1,)),
+            dma((nv // 2 - 1,)),
+            dma((nv // 2 - 1,)),
             dma((2,)),
             dma((2,)),
             dma((levels - 1, views)),
@@ -804,12 +838,14 @@
             dma((views, 2 * levels)),
             dma((views, 2 * levels)),
             dma((views, 2 * levels)),
-            dma((views, nv - 1)),
-            dma((views, nv - 1)),
+            dma((views, nv // 2 - 1)),
+            dma((views, nv // 2 - 1)),
             dma((2,)),
             dma((2,)),
-            dma((7, 2, 2)),
-            dma((7, 2, 2)),
+            dma((2,)),
+            dma((2,)),
+            dma((7, 2, 3)),
+            dma((7, 2, 3)),
         ],
         compiler_params=pltpu.CompilerParams(
             collective_id=0, has_side_effects=True, vmem_limit_bytes=FRONT_VMEM * MIB

time: 128 us -> 121 us (0.945)
  Pallas kernels: 128 us -> 120 us
    pallas_call x1, Pallas kernels: 121 us -> 114 us  [per_device(): pl.pallas_call(functools.partial(front_kernel, nv, nt), out_shape=(band,...]
where the time goes in v4:
time: 121 us; the launch traced here: 120 us
  Pallas kernels  120 us (99%)
    pallas_call x1, Pallas kernels, per_device(): pl.pallas_call(functools.partial(front_kernel, nv, nt), out_shape=(band,...  114 us
    pallas_call x1, Pallas kernels, per_device(): pl.pallas_call(widen_kernel, out_shape=(band, band, jax.ShapeDtypeStruct(...  6.21 us

profile of v4, /device:TPU:1, one launch (start us, length us, event | category | flops | bytes accessed | tf_op | source)
XLA Modules:
  0.0 120.5 jit_solution(9605065984687981256)
XLA Ops:
  0.6 113.6 %front.1 = (f32[2,2,64,128]{3,2,1,0:T(8,128)}, f32[2,2,64,128]{3,2,1,0:T(8,128)}, bf16[8,2,8,128,128]{4,3,2,1,0:T(8,128)(2,1)}) custom-call(s32[2,32]{1,0:T(2,128)} %positions.1, s32[2]{0:T(128)} %bitcast.2, s32[2]{0:T(128)} %bitcast.3, f32[2,2,64,128]{3,2,1,0:T(8,128)} %object_hbm.1, f32[2,2,64,128]{3,2,1,0:T(8,128)} %dual_hbm.1, f32[2,128,128]{2,1,0:T(8,128)} %probe_hbm.1, ...), custom_call_target="tpu_custom_call" | custom-call | tf_op jit(solution)/shard_map/front/pallas_call | solution.py:786
  114.3 6.2 %widen.1 = (f32[2,2,64,128]{3,2,1,0:T(8,128)}, f32[2,2,64,128]{3,2,1,0:T(8,128)}, f32[2,64,128,128]{3,2,1,0:T(8,128)}) custom-call(f32[2,2,64,128]{3,2,1,0:T(8,128)} %get-tuple-element.6.object_ref, f32[2,2,64,128]{3,2,1,0:T(8,128)} %get-tuple-element.7.dual_ref, bf16[8,2,8,128,128]{4,3,2,1,0:T(8,128)(2,1)} %get-tuple-element.8.gathered), custom_call_target="tpu_custom_call" | custom-call | tf_op jit(solution)/shard_map/widen/pallas_call | solution.py:867

commit v5 on v4

--- a/solution.py
+++ b/solution.py
@@ -13,10 +13,10 @@
 prior_weight = 0.5
 MESH = pl.DeviceIdType.MESH
 BATCH = 4
-PIECE_ROWS = 16
+PIECE_ROWS = 128
 FRONT_VMEM = 60
 WIDEN_VMEM = 60
-PUMP = (16, 6, 1, 2, 4, 4)
+PUMP = (6, 0, 0, 0, 0, 0)
 MIB = 2**20
 
 
@@ -499,12 +499,13 @@
             resid_copy(a, 2 * k, t, level_at(k) * group + place).start()
         relay_copy(a, 0, t).start()
 
-    def relay_resid(a):
+    def forward_resid(a):
         resid_copy(a, 1, beside, beside).wait_recv()
         for k in range(1, levels):
             resid_copy(a, 2 * k + 1, beside, level_at(k) * group + place).start()
         relay_copy(a, 1, beside).start()
-        for lane in range(2, lanes):
+    def relay_resid(a, first):
+        for lane in range(first, lanes, 2):
             source = source_at(lane, t)
             resid_copy(a, lane, source, t).wait_recv()
             relay_copy(a, lane, source).start()
@@ -539,18 +540,25 @@
             rt_copy(a, k, view_at(2 * k)).start()
 
     batches = slots // BATCH
-    for a in range(views):
-        loads[2 + a].wait()
-        run_patches(a, 0, batches)
-        send_update(a)
-        share_sums(a)
+    loads[2].wait()
+    run_patches(0, 0, batches)
+    send_update(0)
+    loads[3].wait()
+    run_patches(1, 0, batches // 2)
+    share_sums(0)
+    run_patches(1, batches // 2, batches)
+    send_update(1)
+    share_sums(1)
     pump_some(PUMP[3])
     for a in range(views):
         finish_object(a)
         send_resid(a)
     pump_some(PUMP[4])
     for a in range(views):
-        relay_resid(a)
+        forward_resid(a)
+    for first in (2, 3):
+        for a in range(views):
+            relay_resid(a, first)
     pump_some(PUMP[5])
     for a in range(views):
         send_windows(a)
@@ -730,30 +738,29 @@
 def widen_kernel(object_ref, dual_ref, gathered, object_out, dual_out, volume_out, low, wide, in_sem, out_sem):
     parts, _, share_cols = gathered.shape[:3]
 
-    def load(i):
-        return pltpu.make_async_copy(gathered.at[i], low.at[i], in_sem.at[i])
-
-    def store(i):
+    def load(i, k):
+        return pltpu.make_async_copy(gathered.at[i, k], low.at[i, k], in_sem.at[i, k])
+
+    def store(i, k):
         return pltpu.make_async_copy(
-            wide.at[i], volume_out.at[:, pl.ds(i * share_cols, share_cols)], out_sem.at[i]
+            wide.at[i, k], volume_out.at[k, pl.ds(i * share_cols, share_cols)], out_sem.at[i, k]
         )
 
     for i in range(parts):
-        load(i).start()
+        for k in range(2):
+            load(i, k).start()
+    for i in range(parts):
+        for k in range(2):
+            load(i, k).wait()
+            wide[i, k, 1 : share_cols - 1] = low[i, k, : share_cols - 2].astype(jnp.float32)
+            wide[i, k, 0] = low[i, k, share_cols - 2].astype(jnp.float32)
+            wide[i, k, share_cols - 1] = low[i, k, share_cols - 1].astype(jnp.float32)
+            store(i, k).start()
     object_out[...] = object_ref[...]
     dual_out[...] = dual_ref[...]
-
-    def step(i, _):
-        load(i).wait()
-        wide[i, :, 1 : share_cols - 1] = low[i, :, : share_cols - 2].astype(jnp.float32)
-        wide[i, :, 0] = low[i, :, share_cols - 2].astype(jnp.float32)
-        wide[i, :, share_cols - 1] = low[i, :, share_cols - 1].astype(jnp.float32)
-        store(i).start()
-        return 0
-
-    lax.fori_loop(0, parts, step, 0)
     for i in range(parts):
-        store(i).wait()
+        for k in range(2):
+            store(i, k).wait()
 
 
 def per_device(
@@ -872,8 +879,8 @@
         scratch_shapes=[
             pltpu.VMEM(gathered.shape, bf16),
             pltpu.VMEM(gathered.shape, f32),
-            dma((nv,)),
-            dma((nv,)),
+            dma((nv, 2)),
+            dma((nv, 2)),
         ],
         compiler_params=pltpu.CompilerParams(vmem_limit_bytes=WIDEN_VMEM * MIB),
         name="widen",

time: 121 us -> 121 us (level)
  no operation moved by 1% of the time
where the time goes in v5:
time: 121 us
  Pallas kernels  120 us (99%)
    pallas_call x1, Pallas kernels, per_device(): pl.pallas_call(functools.partial(front_kernel, nv, nt), out_shape=(band,...  114 us
    pallas_call x1, Pallas kernels, per_device(): pl.pallas_call(widen_kernel, out_shape=(band, band, jax.ShapeDtypeStruct(...  6.21 us

profile of v5, /device:TPU:1, one launch (start us, length us, event | category | flops | bytes accessed | tf_op | source)
XLA Modules:
  0.0 120.6 jit_solution(12148277035757238766)
XLA Ops:
  0.6 113.7 %front.1 = (f32[2,2,64,128]{3,2,1,0:T(8,128)}, f32[2,2,64,128]{3,2,1,0:T(8,128)}, bf16[8,2,8,128,128]{4,3,2,1,0:T(8,128)(2,1)}) custom-call(s32[2,32]{1,0:T(2,128)} %positions.1, s32[2]{0:T(128)} %bitcast.2, s32[2]{0:T(128)} %bitcast.3, f32[2,2,64,128]{3,2,1,0:T(8,128)} %object_hbm.1, f32[2,2,64,128]{3,2,1,0:T(8,128)} %dual_hbm.1, f32[2,128,128]{2,1,0:T(8,128)} %probe_hbm.1, ...), custom_call_target="tpu_custom_call" | custom-call | tf_op jit(solution)/shard_map/front/pallas_call | solution.py:793
  114.4 6.2 %widen.1 = (f32[2,2,64,128]{3,2,1,0:T(8,128)}, f32[2,2,64,128]{3,2,1,0:T(8,128)}, f32[2,64,128,128]{3,2,1,0:T(8,128)}) custom-call(f32[2,2,64,128]{3,2,1,0:T(8,128)} %get-tuple-element.6.object_ref, f32[2,2,64,128]{3,2,1,0:T(8,128)} %get-tuple-element.7.dual_ref, bf16[8,2,8,128,128]{4,3,2,1,0:T(8,128)(2,1)} %get-tuple-element.8.gathered), custom_call_target="tpu_custom_call" | custom-call | tf_op jit(solution)/shard_map/widen/pallas_call | solution.py:874

commit v6 on v4

--- a/solution.py
+++ b/solution.py
@@ -588,15 +588,16 @@
             pair_out.at[part], pair_in.at[part], pair_send.at[part], pair_recv.at[part], over, t
         )
 
-    half_span = span // 2
-    for part in range(2):
-        pair_out[part] = grad[0, :, part * half_span : (part + 1) * half_span].astype(jnp.bfloat16)
+    pair_parts = share_cols // 2
+    part_span = 2 * depth
+    for part in range(pair_parts):
+        pair_out[part] = grad[0, :, part * part_span : (part + 1) * part_span].astype(jnp.bfloat16)
         pair_copy(part).start()
     grad[1] += product(nv // 2 - 1, view_x)
     def take_pair(part):
         pair_copy(part).wait()
-        for c in range(part * share_cols // 2, (part + 1) * share_cols // 2):
-            in_part = c * depth - part * half_span
+        for c in (2 * part, 2 * part + 1):
+            in_part = c * depth - part * part_span
             for k in range(2):
                 both = grad[1, k * rows : (k + 1) * rows, c * depth : (c + 1) * depth] + pair_in[
                     part, k * rows : (k + 1) * rows, in_part : in_part + depth
@@ -621,12 +622,7 @@
     up, down, across = view_at(2), view_at(-2), view_at(4)
     other_up, other_down = lax.rem(over + 2, nv), lax.rem(over - 2 + nv, nv)
     other_across = lax.rem(over + 4, nv)
-    early = share_cols // 2 - 2
-    spans = (
-        pl.ds(0, early),
-        pl.ds(early, share_cols - 2 - early),
-        pl.ds(share_cols - 2, 2),
-    )
+    spans = [pl.ds(2 * part, 2) for part in range(pair_parts)]
     sent = []
 
     def go(copy):
@@ -667,10 +663,12 @@
         )
 
     take_pair(0)
-    for k in range(2):
-        finish_inner(k, 1, early + 1)
-        send_own(k, 0)
-    take_pair(1)
+    for part in range(1, pair_parts - 1):
+        take_pair(part)
+        for k in range(2):
+            finish_inner(k, 2 * part - 1, 2 * part + 1)
+            send_own(k, part - 1)
+    take_pair(pair_parts - 1)
     for k in range(2):
         halo_out[0, k] = half[k, 0].astype(jnp.bfloat16)
         halo_out[1, k] = half[k, share_cols - 1].astype(jnp.bfloat16)
@@ -681,8 +679,8 @@
     for copy in halo_copies:
         copy.start()
     for k in range(2):
-        finish_inner(k, early + 1, share_cols - 1)
-        send_own(k, 1)
+        finish_inner(k, share_cols - 3, share_cols - 1)
+        send_own(k, pair_parts - 2)
     for copy in halo_copies:
         copy.wait()
     has_back = flag((v > 0) | (t > 0))
@@ -696,11 +694,11 @@
             half[k, share_cols - 2],
             halo_in[1, k].astype(jnp.float32) * has_fore,
         )
-        send_own(k, 2)
+        send_own(k, pair_parts - 1)
 
     own_copy = pltpu.make_async_copy(share, gathered.at[v], local_sem.at[5 + views])
     own_copy.start()
-    for part in range(3):
+    for part in range(pair_parts):
         for k in range(2):
             if k == 0:
                 hand_on(down, 0, part, 0, up).wait_recv()
@@ -711,11 +709,11 @@
             hand_on(over, k, part, 2, over).wait_recv()
             go(hand_on(over, k, part, 4, up))
             go(hand_on(over, k, part, 5, down))
-    for part in range(3):
+    for part in range(pair_parts):
         for k in range(2):
             hand_on(across, k, part, 3, up).wait_recv()
             go(hand_on(across, k, part, 6, over))
-    for part in range(3):
+    for part in range(pair_parts):
         hand_on(down, 1, part, 0, up).wait_recv()
         hand_on(up, 0, part, 1, up).wait_recv()
         for k in range(2):
@@ -816,8 +814,8 @@
             pltpu.VMEM((nt, 2, cols, rows), bf16),
             pltpu.VMEM((nv // 2, 2 * rows, views * 2 * cols), bf16),
             pltpu.VMEM((2, 2 * rows, span), f32),
-            pltpu.VMEM((2, 2 * rows, span // 2), bf16),
-            pltpu.VMEM((2, 2 * rows, span // 2), bf16),
+            pltpu.VMEM((share_cols // 2, 2 * rows, 2 * depth), bf16),
+            pltpu.VMEM((share_cols // 2, 2 * rows, 2 * depth), bf16),
             pltpu.VMEM((2, share_cols, depth, rows), f32),
             pltpu.VMEM((2, 2, depth, rows), bf16),
             pltpu.VMEM((2, 2, depth, rows), bf16),
@@ -840,12 +838,12 @@
             dma((views, 2 * levels)),
             dma((views, nv // 2 - 1)),
             dma((views, nv // 2 - 1)),
+            dma((share_cols // 2,)),
+            dma((share_cols // 2,)),
             dma((2,)),
             dma((2,)),
-            dma((2,)),
-            dma((2,)),
-            dma((7, 2, 3)),
-            dma((7, 2, 3)),
+            dma((7, 2, share_cols // 2)),
+            dma((7, 2, share_cols // 2)),
         ],
         compiler_params=pltpu.CompilerParams(
             collective_id=0, has_side_effects=True, vmem_limit_bytes=FRONT_VMEM * MIB

time: 121 us -> 120 us (level)
  no operation moved by 1% of the time
where the time goes in v6:
time: 120 us
  Pallas kernels  119 us (99%)
    pallas_call x1, Pallas kernels, per_device(): pl.pallas_call(functools.partial(front_kernel, nv, nt), out_shape=(band,...  113 us
    pallas_call x1, Pallas kernels, per_device(): pl.pallas_call(widen_kernel, out_shape=(band, band, jax.ShapeDtypeStruct(...  6.21 us

profile of v6, /device:TPU:1, one launch (start us, length us, event | category | flops | bytes accessed | tf_op | source)
XLA Modules:
  0.0 119.5 jit_solution(4478581318250030940)
XLA Ops:
  0.6 112.7 %front.1 = (f32[2,2,64,128]{3,2,1,0:T(8,128)}, f32[2,2,64,128]{3,2,1,0:T(8,128)}, bf16[8,2,8,128,128]{4,3,2,1,0:T(8,128)(2,1)}) custom-call(s32[2,32]{1,0:T(2,128)} %positions.1, s32[2]{0:T(128)} %bitcast.2, s32[2]{0:T(128)} %bitcast.3, f32[2,2,64,128]{3,2,1,0:T(8,128)} %object_hbm.1, f32[2,2,64,128]{3,2,1,0:T(8,128)} %dual_hbm.1, f32[2,128,128]{2,1,0:T(8,128)} %probe_hbm.1, ...), custom_call_target="tpu_custom_call" | custom-call | tf_op jit(solution)/shard_map/front/pallas_call | solution.py:784
  113.3 6.2 %widen.1 = (f32[2,2,64,128]{3,2,1,0:T(8,128)}, f32[2,2,64,128]{3,2,1,0:T(8,128)}, f32[2,64,128,128]{3,2,1,0:T(8,128)}) custom-call(f32[2,2,64,128]{3,2,1,0:T(8,128)} %get-tuple-element.6.object_ref, f32[2,2,64,128]{3,2,1,0:T(8,128)} %get-tuple-element.7.dual_ref, bf16[8,2,8,128,128]{4,3,2,1,0:T(8,128)(2,1)} %get-tuple-element.8.gathered), custom_call_target="tpu_custom_call" | custom-call | tf_op jit(solution)/shard_map/widen/pallas_call | solution.py:865
